TPU v7x, 512 devices: a whole 4x8x8 slice. The times are simulated.
512 devices in a mesh: row: 32 (over x_lo, z, core), tm: 16 (over y, x_hi).
Axes of the slice: x: 4 (x_hi: 2, x_lo: 2; x = x_hi * 2 + x_lo), y: 8, z: 8, core: 2. Of those that a mesh axis runs over, the one named last changes fastest.
Arguments:
- snapshots: float32 [16384, 16384], P('row', 'tm'), may hold values from -40 to 40
- weights: float32 [16384], P('row'), may hold values from 0.25 to 4
- block_delay: int32 [128], P('tm'), may hold values from 0 to 64, as said below
Outputs:
- csd: float32 [128, 2, 128, 128], P('row', None, 'tm')
Inputs may be any that keep to these rules, and one draw needn't show every extreme that they name: `block_delay`: block b starts at snapshot b * 128 plus its delay, counted cyclically over the 16384 snapshots; some block has delay 0 and some has delay 64.
All inputs are finite; a program needn't handle non-finite values.
Results may differ from a plain program's by a relative error of at most 0.004.
Values may be sent and summed in bfloat16 or wider, within the bound.
No kernel may reach another device: no remote copies, remote signals or barrier semaphores. Data moves between devices by JAX's collectives and lax.ppermute only.
A program may use at most 64 MiB of HBM per device.

v0:
```python
import jax
import jax.numpy as jnp
import numpy as np
from jax import lax
from jax.experimental import pallas as pl
from jax.experimental.pallas import tpu as pltpu
from jax.sharding import Mesh
from jax.sharding import PartitionSpec as P

NFFT = 256
NF = 128
HOP = 128
RIM = 192
REACH = 384
STRIP = 256
PAIR = 2
CORES = 2
LANES = 128
VMEM = 24 * 1024 * 1024


def shifted(array, axis, by):
    count = lax.axis_size(axis)
    return lax.ppermute(array, axis, [(i, (i + by) % count) for i in range(count)])


def dft_rows(groups):
    time_index = np.arange(NFFT)
    angles = 2.0 * np.pi * (time_index[:, None] * np.arange(NF)[None, :] % NFFT) / NFFT
    window = np.sin(np.pi * time_index / NFFT) ** 2
    norm = np.sqrt(np.sum(window * window))
    table = np.stack([window[:, None] * np.cos(angles), -window[:, None] * np.sin(angles)])
    table = (table / norm).reshape(2, NFFT, groups, PAIR, NF // groups // PAIR)
    rows = table.transpose(3, 2, 0, 4, 1).reshape(2 * NF, NFFT)
    rows = np.pad(rows, ((0, 0), (0, REACH - NFFT)))
    return jnp.asarray(rows, jnp.float32).astype(jnp.bfloat16)


def fill_pairs(out_ref, rows, table_ref, data_ref, scale_ref):
    targets = out_ref.shape[0]
    scale = scale_ref[:, rows]
    for pair in range(table_ref.shape[0] // 2):
        two = []
        for block in (2 * pair, 2 * pair + 1):
            spectrum = lax.dot_general(
                table_ref[block],
                data_ref[:, block * HOP : block * HOP + REACH],
                (((1,), (1,)), ((), ())),
                preferred_element_type=jnp.float32,
            )
            two.append((spectrum * scale).reshape(targets, -1, data_ref.shape[0]))
        out_ref[:, pair, :, rows] = jnp.concatenate(two, axis=1).astype(jnp.bfloat16)


def rim_kernel(edge_ref, out_ref):
    rows = edge_ref.shape[0]
    out_ref[:rows] = edge_ref[:, :LANES]
    rest = edge_ref[:, LANES:].astype(jnp.float32)
    both = jnp.concatenate([rest[: rows // 2], rest[rows // 2 :]], axis=1)
    out_ref[rows:] = both.astype(jnp.bfloat16)


def packed_rim(edge):
    rows, _ = edge.shape
    whole = pl.BlockSpec(memory_space=pltpu.VMEM)
    return pl.pallas_call(
        rim_kernel,
        in_specs=[whole],
        out_specs=whole,
        out_shape=jax.ShapeDtypeStruct((rows * RIM // LANES, LANES), jnp.bfloat16),
        compiler_params=pltpu.CompilerParams(vmem_limit_bytes=VMEM),
        name="rim",
    )(edge)


def early_kernel(total_rows, delay_ref, table_ref, weight_ref, snap_ref, out_ref, tail_ref, late_table_ref, scale_ref, shifted_ref, data_ref):
    early = 2 * out_ref.shape[1]

    @pl.when(pl.program_id(0) == 0)
    def _():
        table = table_ref[...].astype(jnp.float32)
        for block in range(delay_ref.shape[0]):
            moved = pltpu.roll(table, delay_ref[block], 1).astype(jnp.bfloat16)
            if block < early:
                shifted_ref[block] = moved
            else:
                late_table_ref[block - early] = moved

    data_ref[...] = snap_ref[...].astype(jnp.bfloat16)
    tail_ref[...] = data_ref[:, early * HOP :]
    scale_ref[...] = jnp.sqrt(weight_ref[...] / total_rows)
    fill_pairs(out_ref, slice(None), shifted_ref, data_ref, scale_ref)


def early_spectra(snapshots, weights, block_delay, table, targets, total_rows):
    rows, span = snapshots.shape
    blocks = span // HOP
    early = (span - REACH) // HOP + 1
    lines = 4 * NF // targets
    tail = span - early * HOP
    return pl.pallas_call(
        lambda *refs: early_kernel(total_rows, *refs),
        grid=(rows // STRIP,),
        in_specs=[
            pl.BlockSpec(memory_space=pltpu.SMEM),
            pl.BlockSpec(table.shape, lambda s: (0, 0)),
            pl.BlockSpec((1, STRIP), lambda s: (0, s)),
            pl.BlockSpec((STRIP, span), lambda s: (s, 0)),
        ],
        out_specs=[
            pl.BlockSpec((targets, early // 2, lines, STRIP), lambda s: (0, 0, 0, s)),
            pl.BlockSpec((STRIP, tail), lambda s: (s, 0)),
            pl.BlockSpec((blocks - early,) + table.shape, lambda s: (0, 0, 0)),
            pl.BlockSpec((1, STRIP), lambda s: (0, s)),
        ],
        out_shape=[
            jax.ShapeDtypeStruct((targets, blocks // 2, lines, rows), jnp.bfloat16),
            jax.ShapeDtypeStruct((rows, tail), jnp.bfloat16),
            jax.ShapeDtypeStruct((blocks - early,) + table.shape, jnp.bfloat16),
            jax.ShapeDtypeStruct((1, rows), jnp.float32),
        ],
        scratch_shapes=[
            pltpu.VMEM((early,) + table.shape, jnp.bfloat16),
            pltpu.VMEM((STRIP, span), jnp.bfloat16),
        ],
        compiler_params=pltpu.CompilerParams(vmem_limit_bytes=VMEM),
        cost_estimate=pl.CostEstimate(
            flops=4 * NF * REACH * rows * early,
            bytes_accessed=4 * rows * span + 4 * NF * rows * early,
            transcendentals=0,
        ),
        name="dft_early",
    )(block_delay, table, weights.reshape(1, rows), snapshots)


def late_kernel(table_ref, scale_ref, tail_ref, rim_ref, begun_ref, out_ref, data_ref):
    rows, tail = tail_ref.shape
    strip = data_ref.shape[0]
    rest = rim_ref[rows:].astype(jnp.float32)
    lane = lax.broadcasted_iota(jnp.int32, rest.shape, 1)
    for s in range(rows // strip):
        part = slice(s * strip, (s + 1) * strip)
        mine = rest if s == 0 else pltpu.roll(rest, RIM - LANES, 1)
        mine = jnp.where(lane < RIM - LANES, mine, 0.0).astype(jnp.bfloat16)
        data_ref[:, :tail] = tail_ref[part]
        data_ref[:, tail : tail + LANES] = rim_ref[part]
        data_ref[:, tail + LANES :] = mine
        fill_pairs(out_ref, part, table_ref, data_ref, scale_ref)


def late_spectra(begun, tail, table, scale, rim):
    targets, pairs, lines, rows = begun.shape
    late = table.shape[0]
    whole = pl.BlockSpec(memory_space=pltpu.VMEM)
    return pl.pallas_call(
        late_kernel,
        grid=(1,),
        in_specs=[whole, whole, whole, whole, pl.BlockSpec(memory_space=pl.ANY)],
        out_specs=pl.BlockSpec(
            (targets, late // 2, lines, rows), lambda s: (0, 2 * pairs // late - 1, 0, 0)
        ),
        out_shape=jax.ShapeDtypeStruct(begun.shape, begun.dtype),
        input_output_aliases={4: 0},
        scratch_shapes=[pltpu.VMEM((STRIP, (late - 1) * HOP + REACH), jnp.bfloat16)],
        compiler_params=pltpu.CompilerParams(vmem_limit_bytes=VMEM),
        cost_estimate=pl.CostEstimate(
            flops=4 * NF * REACH * rows * late,
            bytes_accessed=4 * NF * rows * late,
            transcendentals=0,
        ),
        name="dft_late",
    )(table, scale, tail, rim, begun)


def split_quads(mats):
    eights = [m.reshape(m.shape[0] // 8, 8, m.shape[1]) for m in mats]
    upper = lax.broadcasted_iota(jnp.int32, eights[0].shape, 1) < 4
    low, high = [], []
    for a, b in (eights[:2], eights[2:]):
        low.append(jnp.where(upper, a, pltpu.roll(b, 4, 1)))
        high.append(jnp.where(upper, pltpu.roll(a, 4, 1), b))
    return jnp.concatenate(low, axis=1), jnp.concatenate(high, axis=1)


def csd_kernel(got_ref, own_ref, other_ref, sorted_ref):
    halves, lines, every, rows = sorted_ref.shape
    freqs = lines // 2
    sources = got_ref.shape[0] // halves
    step = 4
    some = step * every // sources
    row = lax.broadcasted_iota(jnp.int32, (some * lines, some * lines), 0)
    column = lax.broadcasted_iota(jnp.int32, (some * lines, some * lines), 1)
    part = (row // some) % 2
    freq = row // (2 * some)
    order = ((row % some) * lines + part * freqs + freq == column).astype(jnp.bfloat16)
    for half in range(halves):
        for k in range(sources // step):
            first = half * sources + k * step
            by_line = lax.dot_general(
                order,
                got_ref[first : first + step].reshape(some * lines, rows),
                (((1,), (0,)), ((), ())),
                preferred_element_type=jnp.float32,
            )
            by_line = by_line.astype(jnp.bfloat16).reshape(lines, some, rows)
            sorted_ref[half, :, k * some : (k + 1) * some, :] = by_line
    real, imag = [], []
    for freq in range(freqs):
        power = 0.0
        for half in range(halves):
            both = sorted_ref[half, 2 * freq : 2 * freq + 2].reshape(2 * every, rows)
            power += lax.dot_general(
                both, both, (((1,), (1,)), ((), ())), preferred_element_type=jnp.float32
            )
        real.append(power[:every, :every] + power[every:, every:])
        imag.append(power[:every, every:] - power[every:, :every])
    first_core = lax.axis_index("core") == 0
    for place, quad in ((0, real), (16, imag)):
        low, high = split_quads(quad)
        own_ref[:, place : place + 16, :] = jnp.where(first_core, low, high)
        other = jnp.where(first_core, high, low)
        other_ref[:, place : place + 16, :] = other.astype(jnp.bfloat16)


def cross_power(got):
    sources, pairs, lines, rows = got.shape
    every = sources // PAIR * 2 * pairs
    shape = (every // 8, 2 * lines, every)
    whole = pl.BlockSpec(memory_space=pltpu.VMEM)
    return pl.pallas_call(
        csd_kernel,
        in_specs=[whole],
        out_specs=[whole, whole],
        out_shape=[
            jax.ShapeDtypeStruct(shape, jnp.float32),
            jax.ShapeDtypeStruct(shape, jnp.bfloat16),
        ],
        scratch_shapes=[pltpu.VMEM((PAIR, lines // 2, every, rows), jnp.bfloat16)],
        compiler_params=pltpu.CompilerParams(vmem_limit_bytes=VMEM),
        name="csd",
    )(got)


def total_kernel(got_ref, out_ref, sum_ref):
    own, parts, freqs, _ = out_ref.shape
    sum_ref[...] = jnp.sum(got_ref[...].astype(jnp.float32), axis=1)
    few = freqs // PAIR
    for half in range(PAIR):
        for part in range(parts):
            for freq in range(few):
                for i in range(own):
                    row = (part * few + freq) * own + i
                    place = half * few + freq
                    out_ref[i, part, place : place + 1, :] = sum_ref[half, row : row + 1, :]


def totals(got, freqs):
    halves, _, lines, every = got.shape
    whole = pl.BlockSpec(memory_space=pltpu.VMEM)
    return pl.pallas_call(
        total_kernel,
        in_specs=[whole],
        out_specs=whole,
        out_shape=jax.ShapeDtypeStruct((lines * halves // (2 * freqs), 2, freqs, every), jnp.float32),
        scratch_shapes=[pltpu.VMEM((halves, lines, every), jnp.float32)],
        compiler_params=pltpu.CompilerParams(vmem_limit_bytes=VMEM),
        name="total",
    )(got)


def body(snapshots, weights, block_delay):
    groups = lax.axis_size("tm")
    chips = lax.axis_size("chip")
    targets = PAIR * groups
    total_rows = snapshots.shape[0] * PAIR * chips * CORES

    def exchange(array, axes):
        return lax.all_to_all(array, axes, split_axis=0, concat_axis=0, tiled=True)

    rim = shifted(packed_rim(snapshots[:, :RIM].astype(jnp.bfloat16)), "tm", -1)
    begun = early_spectra(snapshots, weights, block_delay, dft_rows(groups), targets, total_rows)
    spectra = late_spectra(*begun, rim)
    own, other = cross_power(exchange(spectra, ("half", "tm")))
    pair = (own + shifted(other, "core", 1).astype(jnp.float32)).astype(jnp.bfloat16)
    got = exchange(pair, ("half", "chip"))
    return totals(got.reshape((PAIR, chips) + got.shape[1:]), NF // groups)


def solution(mesh):
    rows, groups = mesh.devices.shape
    row = ("half", "chip", "core")
    split = Mesh(
        mesh.devices.reshape(PAIR, rows // PAIR // CORES, CORES, groups), row + ("tm",)
    )
    return jax.shard_map(
        body,
        mesh=split,
        in_specs=(P(row, "tm"), P(row), P("tm")),
        out_specs=P(row, None, "tm", None),
        check_vma=False,
    )
```

profile of v0, /device:TPU:1, one launch (start us, length us, event | category | flops | bytes accessed | tf_op | source)
XLA Modules:
  0.0 96.3 jit_solution(16442010487519171435)
XLA Ops:
  0.0 1.1 %slice.7.edge_ref = bf16[512,192]{1,0:T(8,128)(2,1)S(1)} slice(f32[512,1024]{1,0:T(8,128)} %refs_3_.1), slice={[0:512], [0:192]} | slice | bytes 393216 | tf_op jit(solution)/shard_map/slice | solution.py:280
  1.1 0.1 rim.1
  1.2 8.4 %collective-permute-start = (bf16[768,128]{1,0:T(8,128)(2,1)S(1)}, bf16[768,128]{1,0:T(8,128)(2,1)S(1)}, u32[]{:S(2)}, u32[]{:S(2)}) collective-permute-start(bf16[768,128]{1,0:T(8,128)(2,1)S(1)} %rim.1), channel_id=1, source_target_pairs={{0,15},{1,0},{2,1},{3,2},{4,3},{5,4},{6,5},{7,6},{8,7},{9,8},{10,9... | collective-permute-start | bytes 589832 | tf_op jit(solution)/shard_map/ppermute | solution.py:24
  9.6 0.0 copy-start
  9.6 1.6 %copy-done = f32[512,1024]{1,0:T(8,128)S(1)} copy-done((f32[512,1024]{1,0:T(8,128)S(1)}, f32[512,1024]{1,0:T(8,128)}, u32[]{:S(2)}) %copy-start) | copy-done | bytes 2097176
  11.2 0.0 copy-start.1
  11.2 0.9 copy-done.1
  12.1 0.0 copy-start.2
  12.1 0.7 copy-done.2
  12.8 0.0 copy-start.3
  12.8 0.7 copy-done.3
  13.4 2.7 %dft_early.1 = (bf16[32,4,16,512]{3,2,1,0:T(8,128)(2,1)S(1)}, bf16[512,256]{1,0:T(8,128)(2,1)S(1)}, bf16[2,256,384]{2,1,0:T(8,128)(2,1)S(1)}, f32[1,512]{1,0:T(1,128)S(1)}) custom-call(s32[8]{0:T(128)S(1)} %copy-done.3, bf16[256,384]{1,0:T(8,128)(2,1)S(1)} %copy-done.1, f32[1,512]{1,0:T(1,128)S(1)} %bitcast.3, f32[512,1024]{1,0:T(8,128)S(1)} %copy-done), custom_call_target="tpu_custom_call" | custom-call | flops 603979776 | bytes 3670016 | tf_op jit(solution)/shard_map/dft_early/pallas_call | solution.py:101
  16.1 0.0 collective-permute-done.rim_ref
  16.1 0.5 dft_late.1
  16.6 53.9 %all_to_all.10.got_ref = bf16[32,4,16,512]{3,2,1,0:T(8,128)(2,1)S(1)} all-to-all(bf16[32,4,16,512]{3,2,1,0:T(8,128)(2,1)S(1)} %dft_late.1), channel_id=1, replica_groups=mesh['half'=2,'chip'=8,'core'=2,'tm'=16] {'half','tm'}, dimensions={0} | all-to-all | bytes 4194304 | tf_op jit(solution)/shard_map/all_to_all | solution.py:278
  70.5 1.4 %csd.1 = (f32[16,32,128]{2,1,0:T(8,128)S(1)}, bf16[16,32,128]{2,1,0:T(8,128)(2,1)S(1)}) custom-call(bf16[32,4,16,512]{3,2,1,0:T(8,128)(2,1)S(1)} %all_to_all.10.got_ref), custom_call_target="tpu_custom_call" | custom-call | tf_op jit(solution)/shard_map/csd/pallas_call | solution.py:230
  71.9 5.1 %collective-permute-start.1 = (bf16[16,32,128]{2,1,0:T(8,128)(2,1)S(1)}, bf16[16,32,128]{2,1,0:T(8,128)(2,1)S(1)}, u32[]{:S(2)}, u32[]{:S(2)}) collective-permute-start(bf16[16,32,128]{2,1,0:T(8,128)(2,1)S(1)} %get-tuple-element.16), channel_id=1, source_target_pairs={{0,16},{16,0},{1,17},{17,1},{2,18},{18,2},{3,19},{19,3},{4,20},{20... | collective-permute-start | bytes 393224 | tf_op jit(solution)/shard_map/ppermute | solution.py:24
  77.0 1.0 %collective-permute-done.1 = bf16[16,32,128]{2,1,0:T(8,128)(2,1)S(1)} collective-permute-done((bf16[16,32,128]{2,1,0:T(8,128)(2,1)S(1)}, bf16[16,32,128]{2,1,0:T(8,128)(2,1)S(1)}, u32[]{:S(2)}, u32[]{:S(2)}) %collective-permute-start.1) | collective-permute-done | bytes 131104 | tf_op jit(solution)/shard_map/ppermute | solution.py:24
  78.0 17.6 %all_to_all.11 = bf16[16,32,128]{2,1,0:T(8,128)(2,1)S(1)} all-to-all(bf16[16,32,128]{2,1,0:T(8,128)(2,1)S(1)} %add_convert_fusion), channel_id=1, replica_groups=mesh['half'=2,'chip'=8,'core'=2,'tm'=16] {'half','chip'}, dimensions={0} | all-to-all | bytes 262144 | tf_op jit(solution)/shard_map/all_to_all | solution.py:278
  95.7 0.7 total.1
  (1 shorter events, 0.0 us)
Async XLA Ops:
  1.2 14.9 %collective-permute-start = (bf16[768,128]{1,0:T(8,128)(2,1)S(1)}, bf16[768,128]{1,0:T(8,128)(2,1)S(1)}, u32[]{:S(2)}, u32[]{:S(2)}) collective-permute-start(bf16[768,128]{1,0:T(8,128)(2,1)S(1)} %rim.1), channel_id=1, source_target_pairs={{0,15},{1,0},{2,1},{3,2},{4,3},{5,4},{6,5},{7,6},{8,7},{9,8},{10,9... | collective-permute-start | bytes 589832 | tf_op jit(solution)/shard_map/ppermute | solution.py:24
  9.6 1.6 %copy-start = (f32[512,1024]{1,0:T(8,128)S(1)}, f32[512,1024]{1,0:T(8,128)}, u32[]{:S(2)}) copy-start(f32[512,1024]{1,0:T(8,128)} %refs_3_.1) | copy-start | bytes 6291460
  11.2 0.9 copy-start.1
  12.1 0.7 copy-start.2
  12.8 0.7 copy-start.3
  71.9 6.1 %collective-permute-start.1 = (bf16[16,32,128]{2,1,0:T(8,128)(2,1)S(1)}, bf16[16,32,128]{2,1,0:T(8,128)(2,1)S(1)}, u32[]{:S(2)}, u32[]{:S(2)}) collective-permute-start(bf16[16,32,128]{2,1,0:T(8,128)(2,1)S(1)} %get-tuple-element.16), channel_id=1, source_target_pairs={{0,16},{16,0},{1,17},{17,1},{2,18},{18,2},{3,19},{19,3},{4,20},{20... | collective-permute-start | bytes 393224 | tf_op jit(solution)/shard_map/ppermute | solution.py:24
where the time goes:
time: 96.9 us; the launch traced here: 96.3 us
  blocking collectives  71.5 us (74%)
  starting transfers between devices  13.5 us (14%)
  Pallas kernels  5.3 us (5%)
  local copies, waits for them, and re-layouts  4.92 us (5%)
  waiting for transfers between devices  0.97 us (1%)
    all_to_all x2, blocking collectives, exchange(): return lax.all_to_all(array, axes, split_axis=0, concat_axis=0, tiled=True)  71.5 us
    ppermute x2, starting transfers between devices, shifted(): lax.ppermute(array, axis, [(i, (i + by) % count) for i in range(count)])  13.5 us
    unnamed x8, local copies, waits for them, and re-layouts  3.85 us
    pallas_call x1, Pallas kernels, early_spectra(): pl.pallas_call(lambda *refs: early_kernel(total_rows, *refs), grid=(rows...  2.67 us
  transfers between devices with their start and end apart: 2, of which 1 were waited for; matrix products, arithmetic and copies ran while one was open for 0% of the time, Pallas kernels for 3%

commit v1 on v0

--- a/solution.py
+++ b/solution.py
@@ -15,6 +15,7 @@
 STRIP = 256
 PAIR = 2
 CORES = 2
+SORTED = 256
 LANES = 128
 VMEM = 24 * 1024 * 1024
 
@@ -73,11 +74,21 @@
     )(edge)
 
 
-def early_kernel(total_rows, delay_ref, table_ref, weight_ref, snap_ref, out_ref, tail_ref, late_table_ref, scale_ref, shifted_ref, data_ref):
+def sorting_matrix(size, lines):
+    some, freqs = size // lines, lines // 2
+    row = lax.broadcasted_iota(jnp.int32, (size, size), 0)
+    column = lax.broadcasted_iota(jnp.int32, (size, size), 1)
+    part = (row // some) % 2
+    freq = row // (2 * some)
+    return ((row % some) * lines + part * freqs + freq == column).astype(jnp.bfloat16)
+
+
+def early_kernel(total_rows, delay_ref, table_ref, weight_ref, snap_ref, out_ref, tail_ref, late_table_ref, scale_ref, order_ref, shifted_ref, data_ref):
     early = 2 * out_ref.shape[1]
 
     @pl.when(pl.program_id(0) == 0)
     def _():
+        order_ref[...] = sorting_matrix(order_ref.shape[0], out_ref.shape[2] // 2)
         table = table_ref[...].astype(jnp.float32)
         for block in range(delay_ref.shape[0]):
             moved = pltpu.roll(table, delay_ref[block], 1).astype(jnp.bfloat16)
@@ -112,12 +123,14 @@
             pl.BlockSpec((STRIP, tail), lambda s: (s, 0)),
             pl.BlockSpec((blocks - early,) + table.shape, lambda s: (0, 0, 0)),
             pl.BlockSpec((1, STRIP), lambda s: (0, s)),
+            pl.BlockSpec((SORTED, SORTED), lambda s: (0, 0)),
         ],
         out_shape=[
             jax.ShapeDtypeStruct((targets, blocks // 2, lines, rows), jnp.bfloat16),
             jax.ShapeDtypeStruct((rows, tail), jnp.bfloat16),
             jax.ShapeDtypeStruct((blocks - early,) + table.shape, jnp.bfloat16),
             jax.ShapeDtypeStruct((1, rows), jnp.float32),
+            jax.ShapeDtypeStruct((SORTED, SORTED), jnp.bfloat16),
         ],
         scratch_shapes=[
             pltpu.VMEM((early,) + table.shape, jnp.bfloat16),
@@ -182,36 +195,29 @@
     return jnp.concatenate(low, axis=1), jnp.concatenate(high, axis=1)
 
 
-def csd_kernel(got_ref, own_ref, other_ref, sorted_ref):
-    halves, lines, every, rows = sorted_ref.shape
-    freqs = lines // 2
-    sources = got_ref.shape[0] // halves
-    step = 4
-    some = step * every // sources
-    row = lax.broadcasted_iota(jnp.int32, (some * lines, some * lines), 0)
-    column = lax.broadcasted_iota(jnp.int32, (some * lines, some * lines), 1)
-    part = (row // some) % 2
-    freq = row // (2 * some)
-    order = ((row % some) * lines + part * freqs + freq == column).astype(jnp.bfloat16)
-    for half in range(halves):
+def csd_kernel(order_ref, got_ref, own_ref, other_ref, sorted_ref):
+    lines, every, _ = sorted_ref.shape
+    rows = got_ref.shape[3]
+    sources = got_ref.shape[0] // PAIR
+    some = SORTED // lines
+    step = sources * some // every
+    for half in range(PAIR):
         for k in range(sources // step):
             first = half * sources + k * step
             by_line = lax.dot_general(
-                order,
+                order_ref[...],
                 got_ref[first : first + step].reshape(some * lines, rows),
                 (((1,), (0,)), ((), ())),
                 preferred_element_type=jnp.float32,
             )
             by_line = by_line.astype(jnp.bfloat16).reshape(lines, some, rows)
-            sorted_ref[half, :, k * some : (k + 1) * some, :] = by_line
+            sorted_ref[:, k * some : (k + 1) * some, half * rows : (half + 1) * rows] = by_line
     real, imag = [], []
-    for freq in range(freqs):
-        power = 0.0
-        for half in range(halves):
-            both = sorted_ref[half, 2 * freq : 2 * freq + 2].reshape(2 * every, rows)
-            power += lax.dot_general(
-                both, both, (((1,), (1,)), ((), ())), preferred_element_type=jnp.float32
-            )
+    for freq in range(lines // 2):
+        both = sorted_ref[2 * freq : 2 * freq + 2].reshape(2 * every, PAIR * rows)
+        power = lax.dot_general(
+            both, both, (((1,), (1,)), ((), ())), preferred_element_type=jnp.float32
+        )
         real.append(power[:every, :every] + power[every:, every:])
         imag.append(power[:every, every:] - power[every:, :every])
     first_core = lax.axis_index("core") == 0
@@ -222,23 +228,23 @@
         other_ref[:, place : place + 16, :] = other.astype(jnp.bfloat16)
 
 
-def cross_power(got):
+def cross_power(order, got):
     sources, pairs, lines, rows = got.shape
     every = sources // PAIR * 2 * pairs
     shape = (every // 8, 2 * lines, every)
     whole = pl.BlockSpec(memory_space=pltpu.VMEM)
     return pl.pallas_call(
         csd_kernel,
-        in_specs=[whole],
+        in_specs=[whole, whole],
         out_specs=[whole, whole],
         out_shape=[
             jax.ShapeDtypeStruct(shape, jnp.float32),
             jax.ShapeDtypeStruct(shape, jnp.bfloat16),
         ],
-        scratch_shapes=[pltpu.VMEM((PAIR, lines // 2, every, rows), jnp.bfloat16)],
+        scratch_shapes=[pltpu.VMEM((lines // 2, every, PAIR * rows), jnp.bfloat16)],
         compiler_params=pltpu.CompilerParams(vmem_limit_bytes=VMEM),
         name="csd",
-    )(got)
+    )(order, got)
 
 
 def total_kernel(got_ref, out_ref, sum_ref):
@@ -278,9 +284,11 @@
         return lax.all_to_all(array, axes, split_axis=0, concat_axis=0, tiled=True)
 
     rim = shifted(packed_rim(snapshots[:, :RIM].astype(jnp.bfloat16)), "tm", -1)
-    begun = early_spectra(snapshots, weights, block_delay, dft_rows(groups), targets, total_rows)
+    *begun, order = early_spectra(
+        snapshots, weights, block_delay, dft_rows(groups), targets, total_rows
+    )
     spectra = late_spectra(*begun, rim)
-    own, other = cross_power(exchange(spectra, ("half", "tm")))
+    own, other = cross_power(order, exchange(spectra, ("half", "tm")))
     pair = (own + shifted(other, "core", 1).astype(jnp.float32)).astype(jnp.bfloat16)
     got = exchange(pair, ("half", "chip"))
     return totals(got.reshape((PAIR, chips) + got.shape[1:]), NF // groups)

time: 96.9 us -> 96.8 us (level)
  no operation moved by 1% of the time
where the time goes in v1:
time: 96.8 us; the launch traced here: 96.2 us
  blocking collectives  71.4 us (74%)
  starting transfers between devices  13.5 us (14%)
  Pallas kernels  5.27 us (5%)
  local copies, waits for them, and re-layouts  4.92 us (5%)
  waiting for transfers between devices  0.97 us (1%)
    all_to_all x2, blocking collectives, exchange(): return lax.all_to_all(array, axes, split_axis=0, concat_axis=0, tiled=True)  71.4 us
    ppermute x2, starting transfers between devices, shifted(): lax.ppermute(array, axis, [(i, (i + by) % count) for i in range(count)])  13.5 us
    unnamed x8, local copies, waits for them, and re-layouts  3.85 us
    pallas_call x1, Pallas kernels, early_spectra(): pl.pallas_call(lambda *refs: early_kernel(total_rows, *refs), grid=(rows...  2.75 us
  transfers between devices with their start and end apart: 2, of which 1 were waited for; matrix products, arithmetic and copies ran while one was open for 0% of the time, Pallas kernels for 3%

profile of v1, /device:TPU:1, one launch (start us, length us, event | category | flops | bytes accessed | tf_op | source)
XLA Modules:
  0.0 96.2 jit_solution(5759350291578901831)
XLA Ops:
  0.0 1.1 %slice.7.edge_ref = bf16[512,192]{1,0:T(8,128)(2,1)S(1)} slice(f32[512,1024]{1,0:T(8,128)} %refs_3_.1), slice={[0:512], [0:192]} | slice | bytes 393216 | tf_op jit(solution)/shard_map/slice | solution.py:286
  1.1 0.1 rim.1
  1.2 8.4 %collective-permute-start = (bf16[768,128]{1,0:T(8,128)(2,1)S(1)}, bf16[768,128]{1,0:T(8,128)(2,1)S(1)}, u32[]{:S(2)}, u32[]{:S(2)}) collective-permute-start(bf16[768,128]{1,0:T(8,128)(2,1)S(1)} %rim.1), channel_id=1, source_target_pairs={{0,15},{1,0},{2,1},{3,2},{4,3},{5,4},{6,5},{7,6},{8,7},{9,8},{10,9... | collective-permute-start | bytes 589832 | tf_op jit(solution)/shard_map/ppermute | solution.py:25
  9.6 0.0 copy-start
  9.6 1.6 %copy-done = f32[512,1024]{1,0:T(8,128)S(1)} copy-done((f32[512,1024]{1,0:T(8,128)S(1)}, f32[512,1024]{1,0:T(8,128)}, u32[]{:S(2)}) %copy-start) | copy-done | bytes 2097176
  11.2 0.0 copy-start.1
  11.2 0.9 copy-done.1
  12.1 0.0 copy-start.2
  12.1 0.7 copy-done.2
  12.8 0.0 copy-start.3
  12.8 0.7 copy-done.3
  13.4 2.8 %dft_early.1 = (bf16[32,4,16,512]{3,2,1,0:T(8,128)(2,1)S(1)}, bf16[512,256]{1,0:T(8,128)(2,1)S(1)}, bf16[2,256,384]{2,1,0:T(8,128)(2,1)S(1)}, f32[1,512]{1,0:T(1,128)S(1)}, bf16[256,256]{1,0:T(8,128)(2,1)S(1)}) custom-call(s32[8]{0:T(128)S(1)} %copy-done.3, bf16[256,384]{1,0:T(8,128)(2,1)S(1)} %copy-done.1, f32[1,512]{1,0:T(1,128)S(1)} %bitcast.3, ...), custom_call_target="tpu_custom_call" | custom-call | flops 603979776 | bytes 3670016 | tf_op jit(solution)/shard_map/dft_early/pallas_call | solution.py:112
  16.2 0.0 collective-permute-done.rim_ref
  16.2 0.5 dft_late.1
  16.7 53.8 %all_to_all.10.got_ref = bf16[32,4,16,512]{3,2,1,0:T(8,128)(2,1)S(1)} all-to-all(bf16[32,4,16,512]{3,2,1,0:T(8,128)(2,1)S(1)} %dft_late.1), channel_id=1, replica_groups=mesh['half'=2,'chip'=8,'core'=2,'tm'=16] {'half','tm'}, dimensions={0} | all-to-all | bytes 4194304 | tf_op jit(solution)/shard_map/all_to_all | solution.py:284
  70.5 1.3 %csd.1 = (f32[16,32,128]{2,1,0:T(8,128)S(1)}, bf16[16,32,128]{2,1,0:T(8,128)(2,1)S(1)}) custom-call(bf16[256,256]{1,0:T(8,128)(2,1)S(1)} %get-tuple-element.12.order_ref, bf16[32,4,16,512]{3,2,1,0:T(8,128)(2,1)S(1)} %all_to_all.10.got_ref), custom_call_target="tpu_custom_call" | custom-call | tf_op jit(solution)/shard_map/csd/pallas_call | solution.py:236
  71.8 5.1 %collective-permute-start.1 = (bf16[16,32,128]{2,1,0:T(8,128)(2,1)S(1)}, bf16[16,32,128]{2,1,0:T(8,128)(2,1)S(1)}, u32[]{:S(2)}, u32[]{:S(2)}) collective-permute-start(bf16[16,32,128]{2,1,0:T(8,128)(2,1)S(1)} %get-tuple-element.18), channel_id=1, source_target_pairs={{0,16},{16,0},{1,17},{17,1},{2,18},{18,2},{3,19},{19,3},{4,20},{20... | collective-permute-start | bytes 393224 | tf_op jit(solution)/shard_map/ppermute | solution.py:25
  76.9 1.0 %collective-permute-done.1 = bf16[16,32,128]{2,1,0:T(8,128)(2,1)S(1)} collective-permute-done((bf16[16,32,128]{2,1,0:T(8,128)(2,1)S(1)}, bf16[16,32,128]{2,1,0:T(8,128)(2,1)S(1)}, u32[]{:S(2)}, u32[]{:S(2)}) %collective-permute-start.1) | collective-permute-done | bytes 131104 | tf_op jit(solution)/shard_map/ppermute | solution.py:25
  77.9 17.6 %all_to_all.11 = bf16[16,32,128]{2,1,0:T(8,128)(2,1)S(1)} all-to-all(bf16[16,32,128]{2,1,0:T(8,128)(2,1)S(1)} %add_convert_fusion), channel_id=1, replica_groups=mesh['half'=2,'chip'=8,'core'=2,'tm'=16] {'half','chip'}, dimensions={0} | all-to-all | bytes 262144 | tf_op jit(solution)/shard_map/all_to_all | solution.py:284
  95.5 0.7 total.1
  (1 shorter events, 0.0 us)
Async XLA Ops:
  1.2 15.0 %collective-permute-start = (bf16[768,128]{1,0:T(8,128)(2,1)S(1)}, bf16[768,128]{1,0:T(8,128)(2,1)S(1)}, u32[]{:S(2)}, u32[]{:S(2)}) collective-permute-start(bf16[768,128]{1,0:T(8,128)(2,1)S(1)} %rim.1), channel_id=1, source_target_pairs={{0,15},{1,0},{2,1},{3,2},{4,3},{5,4},{6,5},{7,6},{8,7},{9,8},{10,9... | collective-permute-start | bytes 589832 | tf_op jit(solution)/shard_map/ppermute | solution.py:25
  9.6 1.6 %copy-start = (f32[512,1024]{1,0:T(8,128)S(1)}, f32[512,1024]{1,0:T(8,128)}, u32[]{:S(2)}) copy-start(f32[512,1024]{1,0:T(8,128)} %refs_3_.1) | copy-start | bytes 6291460
  11.2 0.9 copy-start.1
  12.1 0.7 copy-start.2
  12.8 0.7 copy-start.3
  71.8 6.1 %collective-permute-start.1 = (bf16[16,32,128]{2,1,0:T(8,128)(2,1)S(1)}, bf16[16,32,128]{2,1,0:T(8,128)(2,1)S(1)}, u32[]{:S(2)}, u32[]{:S(2)}) collective-permute-start(bf16[16,32,128]{2,1,0:T(8,128)(2,1)S(1)} %get-tuple-element.18), channel_id=1, source_target_pairs={{0,16},{16,0},{1,17},{17,1},{2,18},{18,2},{3,19},{19,3},{4,20},{20... | collective-permute-start | bytes 393224 | tf_op jit(solution)/shard_map/ppermute | solution.py:25

commit v2 on v1

--- a/solution.py
+++ b/solution.py
@@ -32,7 +32,7 @@
     norm = np.sqrt(np.sum(window * window))
     table = np.stack([window[:, None] * np.cos(angles), -window[:, None] * np.sin(angles)])
     table = (table / norm).reshape(2, NFFT, groups, PAIR, NF // groups // PAIR)
-    rows = table.transpose(3, 2, 0, 4, 1).reshape(2 * NF, NFFT)
+    rows = table.transpose(2, 3, 0, 4, 1).reshape(2 * NF, NFFT)
     rows = np.pad(rows, ((0, 0), (0, REACH - NFFT)))
     return jnp.asarray(rows, jnp.float32).astype(jnp.bfloat16)
 
@@ -146,19 +146,24 @@
     )(block_delay, table, weights.reshape(1, rows), snapshots)
 
 
-def late_kernel(table_ref, scale_ref, tail_ref, rim_ref, begun_ref, out_ref, data_ref):
-    rows, tail = tail_ref.shape
-    strip = data_ref.shape[0]
+def late_kernel(table_ref, scale_ref, tail_ref, rim_ref, begun_ref, out_ref):
+    rows, _ = tail_ref.shape
+    half = RIM - LANES
     rest = rim_ref[rows:].astype(jnp.float32)
-    lane = lax.broadcasted_iota(jnp.int32, rest.shape, 1)
-    for s in range(rows // strip):
-        part = slice(s * strip, (s + 1) * strip)
-        mine = rest if s == 0 else pltpu.roll(rest, RIM - LANES, 1)
-        mine = jnp.where(lane < RIM - LANES, mine, 0.0).astype(jnp.bfloat16)
-        data_ref[:, :tail] = tail_ref[part]
-        data_ref[:, tail : tail + LANES] = rim_ref[part]
-        data_ref[:, tail + LANES :] = mine
-        fill_pairs(out_ref, part, table_ref, data_ref, scale_ref)
+    lane = lax.broadcasted_iota(jnp.int32, (rows, LANES), 1)
+    last = jnp.concatenate([rest, pltpu.roll(rest, half, 1)], axis=0)
+    last = jnp.where(lane < half, last, 0.0).astype(jnp.bfloat16)
+    pieces = [tail_ref[:, :HOP], tail_ref[:, HOP:], rim_ref[:rows], last]
+    two = []
+    for block in range(table_ref.shape[0]):
+        products = lax.dot_general(
+            table_ref[block],
+            jnp.concatenate(pieces[block : block + REACH // HOP], axis=1),
+            (((1,), (1,)), ((), ())),
+            preferred_element_type=jnp.float32,
+        )
+        two.append((products * scale_ref[...]).reshape(out_ref.shape[0], -1, rows))
+    out_ref[:, 0] = jnp.concatenate(two, axis=1).astype(jnp.bfloat16)
 
 
 def late_spectra(begun, tail, table, scale, rim):
@@ -174,7 +179,6 @@
         ),
         out_shape=jax.ShapeDtypeStruct(begun.shape, begun.dtype),
         input_output_aliases={4: 0},
-        scratch_shapes=[pltpu.VMEM((STRIP, (late - 1) * HOP + REACH), jnp.bfloat16)],
         compiler_params=pltpu.CompilerParams(vmem_limit_bytes=VMEM),
         cost_estimate=pl.CostEstimate(
             flops=4 * NF * REACH * rows * late,
@@ -197,16 +201,14 @@
 
 def csd_kernel(order_ref, got_ref, own_ref, other_ref, sorted_ref):
     lines, every, _ = sorted_ref.shape
-    rows = got_ref.shape[3]
-    sources = got_ref.shape[0] // PAIR
+    sources, _, _, _, rows = got_ref.shape
     some = SORTED // lines
     step = sources * some // every
     for half in range(PAIR):
         for k in range(sources // step):
-            first = half * sources + k * step
             by_line = lax.dot_general(
                 order_ref[...],
-                got_ref[first : first + step].reshape(some * lines, rows),
+                got_ref[k * step : (k + 1) * step, half].reshape(some * lines, rows),
                 (((1,), (0,)), ((), ())),
                 preferred_element_type=jnp.float32,
             )
@@ -229,8 +231,8 @@
 
 
 def cross_power(order, got):
-    sources, pairs, lines, rows = got.shape
-    every = sources // PAIR * 2 * pairs
+    sources, _, pairs, lines, rows = got.shape
+    every = sources * 2 * pairs
     shape = (every // 8, 2 * lines, every)
     whole = pl.BlockSpec(memory_space=pltpu.VMEM)
     return pl.pallas_call(
@@ -288,7 +290,9 @@
         snapshots, weights, block_delay, dft_rows(groups), targets, total_rows
     )
     spectra = late_spectra(*begun, rim)
-    own, other = cross_power(order, exchange(spectra, ("half", "tm")))
+    received = exchange(spectra, ("tm", "half"))
+    received = received.reshape((groups, PAIR) + received.shape[1:])
+    own, other = cross_power(order, received)
     pair = (own + shifted(other, "core", 1).astype(jnp.float32)).astype(jnp.bfloat16)
     got = exchange(pair, ("half", "chip"))
     return totals(got.reshape((PAIR, chips) + got.shape[1:]), NF // groups)

time: 96.8 us -> 97.4 us (level)
  no operation moved by 1% of the time
where the time goes in v2:
time: 97.4 us; the launch traced here: 96.9 us
  blocking collectives  72 us (74%)
  starting transfers between devices  13.7 us (14%)
  Pallas kernels  5.24 us (5%)
  local copies, waits for them, and re-layouts  4.92 us (5%)
    all_to_all x2, blocking collectives, exchange(): return lax.all_to_all(array, axes, split_axis=0, concat_axis=0, tiled=True)  72 us
    ppermute x2, starting transfers between devices, shifted(): lax.ppermute(array, axis, [(i, (i + by) % count) for i in range(count)])  13.7 us
    unnamed x8, local copies, waits for them, and re-layouts  3.85 us
    pallas_call x1, Pallas kernels, early_spectra(): pl.pallas_call(lambda *refs: early_kernel(total_rows, *refs), grid=(rows...  2.75 us
  transfers between devices with their start and end apart: 2, of which 1 were waited for; matrix products, arithmetic and copies ran while one was open for 0% of the time, Pallas kernels for 3%

profile of v2, /device:TPU:1, one launch (start us, length us, event | category | flops | bytes accessed | tf_op | source)
XLA Modules:
  0.0 96.9 jit_solution(5840602131518792237)
XLA Ops:
  0.0 1.1 %slice.7.edge_ref = bf16[512,192]{1,0:T(8,128)(2,1)S(1)} slice(f32[512,1024]{1,0:T(8,128)} %refs_3_.1), slice={[0:512], [0:192]} | slice | bytes 393216 | tf_op jit(solution)/shard_map/slice | solution.py:288
  1.1 0.1 rim.1
  1.2 8.4 %collective-permute-start = (bf16[768,128]{1,0:T(8,128)(2,1)S(1)}, bf16[768,128]{1,0:T(8,128)(2,1)S(1)}, u32[]{:S(2)}, u32[]{:S(2)}) collective-permute-start(bf16[768,128]{1,0:T(8,128)(2,1)S(1)} %rim.1), channel_id=1, source_target_pairs={{0,15},{1,0},{2,1},{3,2},{4,3},{5,4},{6,5},{7,6},{8,7},{9,8},{10,9... | collective-permute-start | bytes 589832 | tf_op jit(solution)/shard_map/ppermute | solution.py:25
  9.6 0.0 copy-start
  9.6 1.6 %copy-done = f32[512,1024]{1,0:T(8,128)S(1)} copy-done((f32[512,1024]{1,0:T(8,128)S(1)}, f32[512,1024]{1,0:T(8,128)}, u32[]{:S(2)}) %copy-start) | copy-done | bytes 2097176
  11.2 0.0 copy-start.1
  11.2 0.9 copy-done.1
  12.1 0.0 copy-start.2
  12.1 0.7 copy-done.2
  12.8 0.0 copy-start.3
  12.8 0.7 copy-done.3
  13.4 2.8 %dft_early.1 = (bf16[32,4,16,512]{3,2,1,0:T(8,128)(2,1)S(1)}, bf16[512,256]{1,0:T(8,128)(2,1)S(1)}, bf16[2,256,384]{2,1,0:T(8,128)(2,1)S(1)}, f32[1,512]{1,0:T(1,128)S(1)}, bf16[256,256]{1,0:T(8,128)(2,1)S(1)}) custom-call(s32[8]{0:T(128)S(1)} %copy-done.3, bf16[256,384]{1,0:T(8,128)(2,1)S(1)} %copy-done.1, f32[1,512]{1,0:T(1,128)S(1)} %bitcast.5, ...), custom_call_target="tpu_custom_call" | custom-call | flops 603979776 | bytes 3670016 | tf_op jit(solution)/shard_map/dft_early/pallas_call | solution.py:112
  16.2 0.0 collective-permute-done.rim_ref
  16.2 0.5 dft_late.1
  16.7 53.4 %all_to_all.10 = bf16[32,4,16,512]{3,2,1,0:T(8,128)(2,1)S(1)} all-to-all(bf16[32,4,16,512]{3,2,1,0:T(8,128)(2,1)S(1)} %dft_late.1), channel_id=1, replica_groups=mesh['half'=2,'chip'=8,'core'=2,'tm'=16] {'tm','half'}, dimensions={0} | all-to-all | bytes 4194304 | tf_op jit(solution)/shard_map/all_to_all | solution.py:286
  70.1 1.3 %csd.1 = (f32[16,32,128]{2,1,0:T(8,128)S(1)}, bf16[16,32,128]{2,1,0:T(8,128)(2,1)S(1)}) custom-call(bf16[256,256]{1,0:T(8,128)(2,1)S(1)} %get-tuple-element.12.order_ref, bf16[16,2,4,16,512]{4,3,2,1,0:T(8,128)(2,1)S(1)} %bitcast.3), custom_call_target="tpu_custom_call" | custom-call | tf_op jit(solution)/shard_map/csd/pallas_call | solution.py:238
  71.4 5.3 %collective-permute-start.1 = (bf16[16,32,128]{2,1,0:T(8,128)(2,1)S(1)}, bf16[16,32,128]{2,1,0:T(8,128)(2,1)S(1)}, u32[]{:S(2)}, u32[]{:S(2)}) collective-permute-start(bf16[16,32,128]{2,1,0:T(8,128)(2,1)S(1)} %get-tuple-element.18), channel_id=1, source_target_pairs={{0,16},{16,0},{1,17},{17,1},{2,18},{18,2},{3,19},{19,3},{4,20},{20... | collective-permute-start | bytes 393224 | tf_op jit(solution)/shard_map/ppermute | solution.py:25
  76.7 1.0 collective-permute-done.1
  77.7 18.6 %all_to_all.11 = bf16[16,32,128]{2,1,0:T(8,128)(2,1)S(1)} all-to-all(bf16[16,32,128]{2,1,0:T(8,128)(2,1)S(1)} %add_convert_fusion), channel_id=1, replica_groups=mesh['half'=2,'chip'=8,'core'=2,'tm'=16] {'half','chip'}, dimensions={0} | all-to-all | bytes 262144 | tf_op jit(solution)/shard_map/all_to_all | solution.py:286
  96.3 0.7 total.1
  (1 shorter events, 0.0 us)
Async XLA Ops:
  1.2 15.0 %collective-permute-start = (bf16[768,128]{1,0:T(8,128)(2,1)S(1)}, bf16[768,128]{1,0:T(8,128)(2,1)S(1)}, u32[]{:S(2)}, u32[]{:S(2)}) collective-permute-start(bf16[768,128]{1,0:T(8,128)(2,1)S(1)} %rim.1), channel_id=1, source_target_pairs={{0,15},{1,0},{2,1},{3,2},{4,3},{5,4},{6,5},{7,6},{8,7},{9,8},{10,9... | collective-permute-start | bytes 589832 | tf_op jit(solution)/shard_map/ppermute | solution.py:25
  9.6 1.6 %copy-start = (f32[512,1024]{1,0:T(8,128)S(1)}, f32[512,1024]{1,0:T(8,128)}, u32[]{:S(2)}) copy-start(f32[512,1024]{1,0:T(8,128)} %refs_3_.1) | copy-start | bytes 6291460
  11.2 0.9 copy-start.1
  12.1 0.7 copy-start.2
  12.8 0.7 copy-start.3
  71.4 6.3 %collective-permute-start.1 = (bf16[16,32,128]{2,1,0:T(8,128)(2,1)S(1)}, bf16[16,32,128]{2,1,0:T(8,128)(2,1)S(1)}, u32[]{:S(2)}, u32[]{:S(2)}) collective-permute-start(bf16[16,32,128]{2,1,0:T(8,128)(2,1)S(1)} %get-tuple-element.18), channel_id=1, source_target_pairs={{0,16},{16,0},{1,17},{17,1},{2,18},{18,2},{3,19},{19,3},{4,20},{20... | collective-permute-start | bytes 393224 | tf_op jit(solution)/shard_map/ppermute | solution.py:25

commit v3 on v0

--- a/solution.py
+++ b/solution.py
@@ -54,9 +54,11 @@
 
 def rim_kernel(edge_ref, out_ref):
     rows = edge_ref.shape[0]
-    out_ref[:rows] = edge_ref[:, :LANES]
-    rest = edge_ref[:, LANES:].astype(jnp.float32)
-    both = jnp.concatenate([rest[: rows // 2], rest[rows // 2 :]], axis=1)
+    out_ref[:rows] = edge_ref[:, :LANES].astype(jnp.bfloat16)
+    rest = edge_ref[:, LANES:]
+    half = RIM - LANES
+    lane = lax.broadcasted_iota(jnp.int32, (rows // 2, LANES), 1)
+    both = jnp.where(lane < half, rest[: rows // 2], pltpu.roll(rest[rows // 2 :], half, 1))
     out_ref[rows:] = both.astype(jnp.bfloat16)
 
 
@@ -277,7 +279,7 @@
     def exchange(array, axes):
         return lax.all_to_all(array, axes, split_axis=0, concat_axis=0, tiled=True)
 
-    rim = shifted(packed_rim(snapshots[:, :RIM].astype(jnp.bfloat16)), "tm", -1)
+    rim = shifted(packed_rim(snapshots[:, : 2 * LANES]), "tm", -1)
     begun = early_spectra(snapshots, weights, block_delay, dft_rows(groups), targets, total_rows)
     spectra = late_spectra(*begun, rim)
     own, other = cross_power(exchange(spectra, ("half", "tm")))

time: 96.9 us -> 96.9 us (level)
  no operation moved by 1% of the time
where the time goes in v3:
time: 96.9 us; the launch traced here: 96.3 us
  blocking collectives  71.5 us (74%)
  starting transfers between devices  13.5 us (14%)
  Pallas kernels  5.3 us (5%)
  local copies, waits for them, and re-layouts  4.92 us (5%)
  waiting for transfers between devices  0.97 us (1%)
    all_to_all x2, blocking collectives, exchange(): return lax.all_to_all(array, axes, split_axis=0, concat_axis=0, tiled=True)  71.5 us
    ppermute x2, starting transfers between devices, shifted(): lax.ppermute(array, axis, [(i, (i + by) % count) for i in range(count)])  13.5 us
    unnamed x8, local copies, waits for them, and re-layouts  3.85 us
    pallas_call x1, Pallas kernels, early_spectra(): pl.pallas_call(lambda *refs: early_kernel(total_rows, *refs), grid=(rows...  2.67 us
  transfers between devices with their start and end apart: 2, of which 1 were waited for; matrix products, arithmetic and copies ran while one was open for 0% of the time, Pallas kernels for 3%

profile of v3, /device:TPU:1, one launch (start us, length us, event | category | flops | bytes accessed | tf_op | source)
XLA Modules:
  0.0 96.3 jit_solution(15662440384987519939)
XLA Ops:
  0.0 1.1 %slice.3.edge_ref = f32[512,256]{1,0:T(8,128)S(1)} slice(f32[512,1024]{1,0:T(8,128)} %refs_3_.1), slice={[0:512], [0:256]} | slice | bytes 1048576 | tf_op jit(solution)/shard_map/slice | solution.py:282
  1.1 0.1 rim.1
  1.2 8.4 %collective-permute-start = (bf16[768,128]{1,0:T(8,128)(2,1)S(1)}, bf16[768,128]{1,0:T(8,128)(2,1)S(1)}, u32[]{:S(2)}, u32[]{:S(2)}) collective-permute-start(bf16[768,128]{1,0:T(8,128)(2,1)S(1)} %rim.1), channel_id=1, source_target_pairs={{0,15},{1,0},{2,1},{3,2},{4,3},{5,4},{6,5},{7,6},{8,7},{9,8},{10,9... | collective-permute-start | bytes 589832 | tf_op jit(solution)/shard_map/ppermute | solution.py:24
  9.6 0.0 copy-start
  9.6 1.6 %copy-done = f32[512,1024]{1,0:T(8,128)S(1)} copy-done((f32[512,1024]{1,0:T(8,128)S(1)}, f32[512,1024]{1,0:T(8,128)}, u32[]{:S(2)}) %copy-start) | copy-done | bytes 2097176
  11.2 0.0 copy-start.1
  11.2 0.9 copy-done.1
  12.1 0.0 copy-start.2
  12.1 0.7 copy-done.2
  12.8 0.0 copy-start.3
  12.8 0.7 copy-done.3
  13.4 2.7 %dft_early.1 = (bf16[32,4,16,512]{3,2,1,0:T(8,128)(2,1)S(1)}, bf16[512,256]{1,0:T(8,128)(2,1)S(1)}, bf16[2,256,384]{2,1,0:T(8,128)(2,1)S(1)}, f32[1,512]{1,0:T(1,128)S(1)}) custom-call(s32[8]{0:T(128)S(1)} %copy-done.3, bf16[256,384]{1,0:T(8,128)(2,1)S(1)} %copy-done.1, f32[1,512]{1,0:T(1,128)S(1)} %bitcast.3, f32[512,1024]{1,0:T(8,128)S(1)} %copy-done), custom_call_target="tpu_custom_call" | custom-call | flops 603979776 | bytes 3670016 | tf_op jit(solution)/shard_map/dft_early/pallas_call | solution.py:103
  16.1 0.0 collective-permute-done.rim_ref
  16.1 0.5 dft_late.1
  16.6 53.9 %all_to_all.10.got_ref = bf16[32,4,16,512]{3,2,1,0:T(8,128)(2,1)S(1)} all-to-all(bf16[32,4,16,512]{3,2,1,0:T(8,128)(2,1)S(1)} %dft_late.1), channel_id=1, replica_groups=mesh['half'=2,'chip'=8,'core'=2,'tm'=16] {'half','tm'}, dimensions={0} | all-to-all | bytes 4194304 | tf_op jit(solution)/shard_map/all_to_all | solution.py:280
  70.5 1.4 %csd.1 = (f32[16,32,128]{2,1,0:T(8,128)S(1)}, bf16[16,32,128]{2,1,0:T(8,128)(2,1)S(1)}) custom-call(bf16[32,4,16,512]{3,2,1,0:T(8,128)(2,1)S(1)} %all_to_all.10.got_ref), custom_call_target="tpu_custom_call" | custom-call | tf_op jit(solution)/shard_map/csd/pallas_call | solution.py:232
  71.9 5.1 %collective-permute-start.1 = (bf16[16,32,128]{2,1,0:T(8,128)(2,1)S(1)}, bf16[16,32,128]{2,1,0:T(8,128)(2,1)S(1)}, u32[]{:S(2)}, u32[]{:S(2)}) collective-permute-start(bf16[16,32,128]{2,1,0:T(8,128)(2,1)S(1)} %get-tuple-element.16), channel_id=1, source_target_pairs={{0,16},{16,0},{1,17},{17,1},{2,18},{18,2},{3,19},{19,3},{4,20},{20... | collective-permute-start | bytes 393224 | tf_op jit(solution)/shard_map/ppermute | solution.py:24
  77.1 1.0 %collective-permute-done.1 = bf16[16,32,128]{2,1,0:T(8,128)(2,1)S(1)} collective-permute-done((bf16[16,32,128]{2,1,0:T(8,128)(2,1)S(1)}, bf16[16,32,128]{2,1,0:T(8,128)(2,1)S(1)}, u32[]{:S(2)}, u32[]{:S(2)}) %collective-permute-start.1) | collective-permute-done | bytes 131104 | tf_op jit(solution)/shard_map/ppermute | solution.py:24
  78.1 17.6 %all_to_all.11 = bf16[16,32,128]{2,1,0:T(8,128)(2,1)S(1)} all-to-all(bf16[16,32,128]{2,1,0:T(8,128)(2,1)S(1)} %add_convert_fusion), channel_id=1, replica_groups=mesh['half'=2,'chip'=8,'core'=2,'tm'=16] {'half','chip'}, dimensions={0} | all-to-all | bytes 262144 | tf_op jit(solution)/shard_map/all_to_all | solution.py:280
  95.7 0.7 total.1
  (1 shorter events, 0.0 us)
Async XLA Ops:
  1.2 14.9 %collective-permute-start = (bf16[768,128]{1,0:T(8,128)(2,1)S(1)}, bf16[768,128]{1,0:T(8,128)(2,1)S(1)}, u32[]{:S(2)}, u32[]{:S(2)}) collective-permute-start(bf16[768,128]{1,0:T(8,128)(2,1)S(1)} %rim.1), channel_id=1, source_target_pairs={{0,15},{1,0},{2,1},{3,2},{4,3},{5,4},{6,5},{7,6},{8,7},{9,8},{10,9... | collective-permute-start | bytes 589832 | tf_op jit(solution)/shard_map/ppermute | solution.py:24
  9.6 1.6 %copy-start = (f32[512,1024]{1,0:T(8,128)S(1)}, f32[512,1024]{1,0:T(8,128)}, u32[]{:S(2)}) copy-start(f32[512,1024]{1,0:T(8,128)} %refs_3_.1) | copy-start | bytes 6291460
  11.2 0.9 copy-start.1
  12.1 0.7 copy-start.2
  12.8 0.7 copy-start.3
  71.9 6.1 %collective-permute-start.1 = (bf16[16,32,128]{2,1,0:T(8,128)(2,1)S(1)}, bf16[16,32,128]{2,1,0:T(8,128)(2,1)S(1)}, u32[]{:S(2)}, u32[]{:S(2)}) collective-permute-start(bf16[16,32,128]{2,1,0:T(8,128)(2,1)S(1)} %get-tuple-element.16), channel_id=1, source_target_pairs={{0,16},{16,0},{1,17},{17,1},{2,18},{18,2},{3,19},{19,3},{4,20},{20... | collective-permute-start | bytes 393224 | tf_op jit(solution)/shard_map/ppermute | solution.py:24

commit v4 on v2

--- a/solution.py
+++ b/solution.py
@@ -12,7 +12,6 @@
 HOP = 128
 RIM = 192
 REACH = 384
-STRIP = 256
 PAIR = 2
 CORES = 2
 SORTED = 256
@@ -83,58 +82,48 @@
     return ((row % some) * lines + part * freqs + freq == column).astype(jnp.bfloat16)
 
 
-def early_kernel(total_rows, delay_ref, table_ref, weight_ref, snap_ref, out_ref, tail_ref, late_table_ref, scale_ref, order_ref, shifted_ref, data_ref):
+def early_kernel(delay_ref, table_ref, scale_ref, snap_ref, out_ref, tail_ref, late_table_ref, order_ref, shifted_ref, data_ref):
     early = 2 * out_ref.shape[1]
 
-    @pl.when(pl.program_id(0) == 0)
-    def _():
-        order_ref[...] = sorting_matrix(order_ref.shape[0], out_ref.shape[2] // 2)
-        table = table_ref[...].astype(jnp.float32)
-        for block in range(delay_ref.shape[0]):
-            moved = pltpu.roll(table, delay_ref[block], 1).astype(jnp.bfloat16)
-            if block < early:
-                shifted_ref[block] = moved
-            else:
-                late_table_ref[block - early] = moved
-
+    order_ref[...] = sorting_matrix(order_ref.shape[0], out_ref.shape[2] // 2)
+    table = table_ref[...].astype(jnp.float32)
+    for block in range(delay_ref.shape[0]):
+        moved = pltpu.roll(table, delay_ref[block], 1).astype(jnp.bfloat16)
+        if block < early:
+            shifted_ref[block] = moved
+        else:
+            late_table_ref[block - early] = moved
     data_ref[...] = snap_ref[...].astype(jnp.bfloat16)
     tail_ref[...] = data_ref[:, early * HOP :]
-    scale_ref[...] = jnp.sqrt(weight_ref[...] / total_rows)
     fill_pairs(out_ref, slice(None), shifted_ref, data_ref, scale_ref)
 
 
-def early_spectra(snapshots, weights, block_delay, table, targets, total_rows):
+def early_spectra(snapshots, scale, block_delay, table, targets):
     rows, span = snapshots.shape
     blocks = span // HOP
     early = (span - REACH) // HOP + 1
     lines = 4 * NF // targets
     tail = span - early * HOP
-    return pl.pallas_call(
-        lambda *refs: early_kernel(total_rows, *refs),
-        grid=(rows // STRIP,),
-        in_specs=[
-            pl.BlockSpec(memory_space=pltpu.SMEM),
-            pl.BlockSpec(table.shape, lambda s: (0, 0)),
-            pl.BlockSpec((1, STRIP), lambda s: (0, s)),
-            pl.BlockSpec((STRIP, span), lambda s: (s, 0)),
-        ],
+    whole = pl.BlockSpec(memory_space=pltpu.VMEM)
+    return pl.pallas_call(
+        early_kernel,
+        grid=(1,),
+        in_specs=[pl.BlockSpec(memory_space=pltpu.SMEM), whole, whole, whole],
         out_specs=[
-            pl.BlockSpec((targets, early // 2, lines, STRIP), lambda s: (0, 0, 0, s)),
-            pl.BlockSpec((STRIP, tail), lambda s: (s, 0)),
-            pl.BlockSpec((blocks - early,) + table.shape, lambda s: (0, 0, 0)),
-            pl.BlockSpec((1, STRIP), lambda s: (0, s)),
-            pl.BlockSpec((SORTED, SORTED), lambda s: (0, 0)),
+            pl.BlockSpec((targets, early // 2, lines, rows), lambda s: (0, 0, 0, 0)),
+            whole,
+            whole,
+            whole,
         ],
         out_shape=[
             jax.ShapeDtypeStruct((targets, blocks // 2, lines, rows), jnp.bfloat16),
             jax.ShapeDtypeStruct((rows, tail), jnp.bfloat16),
             jax.ShapeDtypeStruct((blocks - early,) + table.shape, jnp.bfloat16),
-            jax.ShapeDtypeStruct((1, rows), jnp.float32),
             jax.ShapeDtypeStruct((SORTED, SORTED), jnp.bfloat16),
         ],
         scratch_shapes=[
             pltpu.VMEM((early,) + table.shape, jnp.bfloat16),
-            pltpu.VMEM((STRIP, span), jnp.bfloat16),
+            pltpu.VMEM((rows, span), jnp.bfloat16),
         ],
         compiler_params=pltpu.CompilerParams(vmem_limit_bytes=VMEM),
         cost_estimate=pl.CostEstimate(
@@ -143,7 +132,7 @@
             transcendentals=0,
         ),
         name="dft_early",
-    )(block_delay, table, weights.reshape(1, rows), snapshots)
+    )(block_delay, table, scale, snapshots)
 
 
 def late_kernel(table_ref, scale_ref, tail_ref, rim_ref, begun_ref, out_ref):
@@ -286,10 +275,11 @@
         return lax.all_to_all(array, axes, split_axis=0, concat_axis=0, tiled=True)
 
     rim = shifted(packed_rim(snapshots[:, :RIM].astype(jnp.bfloat16)), "tm", -1)
-    *begun, order = early_spectra(
-        snapshots, weights, block_delay, dft_rows(groups), targets, total_rows
+    scale = jnp.sqrt(weights / total_rows).reshape(1, -1)
+    begun, tail, table, order = early_spectra(
+        snapshots, scale, block_delay, dft_rows(groups), targets
     )
-    spectra = late_spectra(*begun, rim)
+    spectra = late_spectra(begun, tail, table, scale, rim)
     received = exchange(spectra, ("tm", "half"))
     received = received.reshape((groups, PAIR) + received.shape[1:])
     own, other = cross_power(order, received)

time: 97.4 us -> 97.4 us (level)
    unnamed x8 -> x6, local copies, waits for them, and re-layouts: 3.85 us -> 3.18 us
  transfers between devices with their start and end apart: 2 -> 2, of which waited for: 1 -> 1; matrix products, arithmetic and copies ran while one was open for 0% -> 1% of each run, Pallas kernels for 3% -> 2%
where the time goes in v4:
time: 97.4 us; the launch traced here: 96.9 us
  blocking collectives  72.9 us (75%)
  starting transfers between devices  13.7 us (14%)
  Pallas kernels  4.38 us (4%)
  local copies, waits for them, and re-layouts  4.24 us (4%)
    all_to_all x2, blocking collectives, exchange(): return lax.all_to_all(array, axes, split_axis=0, concat_axis=0, tiled=True)  72.9 us
    ppermute x2, starting transfers between devices, shifted(): lax.ppermute(array, axis, [(i, (i + by) % count) for i in range(count)])  13.7 us
    unnamed x6, local copies, waits for them, and re-layouts  3.18 us
  transfers between devices with their start and end apart: 2, of which 1 were waited for; matrix products, arithmetic and copies ran while one was open for 1% of the time, Pallas kernels for 2%

profile of v4, /device:TPU:1, one launch (start us, length us, event | category | flops | bytes accessed | tf_op | source)
XLA Modules:
  0.0 96.9 jit_solution(11624310579202237269)
XLA Ops:
  0.0 1.1 %slice.7.edge_ref = bf16[512,192]{1,0:T(8,128)(2,1)S(1)} slice(f32[512,1024]{1,0:T(8,128)} %snap_ref.1), slice={[0:512], [0:192]} | slice | bytes 393216 | tf_op jit(solution)/shard_map/slice | solution.py:277
  1.1 0.1 rim.1
  1.2 8.4 %collective-permute-start = (bf16[768,128]{1,0:T(8,128)(2,1)S(1)}, bf16[768,128]{1,0:T(8,128)(2,1)S(1)}, u32[]{:S(2)}, u32[]{:S(2)}) collective-permute-start(bf16[768,128]{1,0:T(8,128)(2,1)S(1)} %rim.1), channel_id=1, source_target_pairs={{0,15},{1,0},{2,1},{3,2},{4,3},{5,4},{6,5},{7,6},{8,7},{9,8},{10,9... | collective-permute-start | bytes 589832 | tf_op jit(solution)/shard_map/ppermute | solution.py:24
  9.6 0.7 multiply_sqrt_fusion
  10.2 0.0 copy-start
  10.3 1.6 %copy-done = f32[512,1024]{1,0:T(8,128)S(1)} copy-done((f32[512,1024]{1,0:T(8,128)S(1)}, f32[512,1024]{1,0:T(8,128)}, u32[]{:S(2)}) %copy-start) | copy-done | bytes 2097176
  11.8 0.0 copy-start.1
  11.8 0.9 copy-done.1
  12.8 0.0 copy-start.2
  12.8 0.7 copy-done.2
  13.4 1.9 %dft_early.1 = (bf16[32,4,16,512]{3,2,1,0:T(8,128)(2,1)S(1)}, bf16[512,256]{1,0:T(8,128)(2,1)S(1)}, bf16[2,256,384]{2,1,0:T(8,128)(2,1)S(1)}, bf16[256,256]{1,0:T(8,128)(2,1)S(1)}) custom-call(s32[8]{0:T(128)S(1)} %copy-done.2, bf16[256,384]{1,0:T(8,128)(2,1)S(1)} %copy-done.1, f32[1,512]{1,0:T(1,128)S(1)} %bitcast.5, f32[512,1024]{1,0:T(8,128)S(1)} %copy-done), custom_call_target="tpu_custom_call" | custom-call | flops 603979776 | bytes 3670016 | tf_op jit(solution)/shard_map/dft_early/pallas_call | solution.py:108
  15.3 0.0 collective-permute-done.rim_ref
  15.3 0.5 dft_late.1
  15.8 54.3 %all_to_all.10 = bf16[32,4,16,512]{3,2,1,0:T(8,128)(2,1)S(1)} all-to-all(bf16[32,4,16,512]{3,2,1,0:T(8,128)(2,1)S(1)} %dft_late.1), channel_id=1, replica_groups=mesh['half'=2,'chip'=8,'core'=2,'tm'=16] {'tm','half'}, dimensions={0} | all-to-all | bytes 4194304 | tf_op jit(solution)/shard_map/all_to_all | solution.py:275
  70.1 1.3 %csd.1 = (f32[16,32,128]{2,1,0:T(8,128)S(1)}, bf16[16,32,128]{2,1,0:T(8,128)(2,1)S(1)}) custom-call(bf16[256,256]{1,0:T(8,128)(2,1)S(1)} %get-tuple-element.11.order_ref, bf16[16,2,4,16,512]{4,3,2,1,0:T(8,128)(2,1)S(1)} %bitcast.3), custom_call_target="tpu_custom_call" | custom-call | tf_op jit(solution)/shard_map/csd/pallas_call | solution.py:227
  71.4 5.3 %collective-permute-start.1 = (bf16[16,32,128]{2,1,0:T(8,128)(2,1)S(1)}, bf16[16,32,128]{2,1,0:T(8,128)(2,1)S(1)}, u32[]{:S(2)}, u32[]{:S(2)}) collective-permute-start(bf16[16,32,128]{2,1,0:T(8,128)(2,1)S(1)} %get-tuple-element.16), channel_id=1, source_target_pairs={{0,16},{16,0},{1,17},{17,1},{2,18},{18,2},{3,19},{19,3},{4,20},{20... | collective-permute-start | bytes 393224 | tf_op jit(solution)/shard_map/ppermute | solution.py:24
  76.7 1.0 collective-permute-done.1
  77.7 18.6 %all_to_all.11 = bf16[16,32,128]{2,1,0:T(8,128)(2,1)S(1)} all-to-all(bf16[16,32,128]{2,1,0:T(8,128)(2,1)S(1)} %add_convert_fusion), channel_id=1, replica_groups=mesh['half'=2,'chip'=8,'core'=2,'tm'=16] {'half','chip'}, dimensions={0} | all-to-all | bytes 262144 | tf_op jit(solution)/shard_map/all_to_all | solution.py:275
  96.3 0.7 total.1
  (1 shorter events, 0.0 us)
Async XLA Ops:
  1.2 14.2 %collective-permute-start = (bf16[768,128]{1,0:T(8,128)(2,1)S(1)}, bf16[768,128]{1,0:T(8,128)(2,1)S(1)}, u32[]{:S(2)}, u32[]{:S(2)}) collective-permute-start(bf16[768,128]{1,0:T(8,128)(2,1)S(1)} %rim.1), channel_id=1, source_target_pairs={{0,15},{1,0},{2,1},{3,2},{4,3},{5,4},{6,5},{7,6},{8,7},{9,8},{10,9... | collective-permute-start | bytes 589832 | tf_op jit(solution)/shard_map/ppermute | solution.py:24
  10.2 1.6 %copy-start = (f32[512,1024]{1,0:T(8,128)S(1)}, f32[512,1024]{1,0:T(8,128)}, u32[]{:S(2)}) copy-start(f32[512,1024]{1,0:T(8,128)} %snap_ref.1) | copy-start | bytes 6291460
  11.8 0.9 copy-start.1
  12.8 0.7 copy-start.2
  71.4 6.3 %collective-permute-start.1 = (bf16[16,32,128]{2,1,0:T(8,128)(2,1)S(1)}, bf16[16,32,128]{2,1,0:T(8,128)(2,1)S(1)}, u32[]{:S(2)}, u32[]{:S(2)}) collective-permute-start(bf16[16,32,128]{2,1,0:T(8,128)(2,1)S(1)} %get-tuple-element.16), channel_id=1, source_target_pairs={{0,16},{16,0},{1,17},{17,1},{2,18},{18,2},{3,19},{19,3},{4,20},{20... | collective-permute-start | bytes 393224 | tf_op jit(solution)/shard_map/ppermute | solution.py:24

commit v5 on v0

--- a/solution.py
+++ b/solution.py
@@ -182,7 +182,7 @@
     return jnp.concatenate(low, axis=1), jnp.concatenate(high, axis=1)
 
 
-def csd_kernel(got_ref, own_ref, other_ref, sorted_ref):
+def csd_kernel(got_ref, out_ref, sorted_ref):
     halves, lines, every, rows = sorted_ref.shape
     freqs = lines // 2
     sources = got_ref.shape[0] // halves
@@ -214,27 +214,22 @@
             )
         real.append(power[:every, :every] + power[every:, every:])
         imag.append(power[:every, every:] - power[every:, :every])
-    first_core = lax.axis_index("core") == 0
     for place, quad in ((0, real), (16, imag)):
         low, high = split_quads(quad)
-        own_ref[:, place : place + 16, :] = jnp.where(first_core, low, high)
-        other = jnp.where(first_core, high, low)
-        other_ref[:, place : place + 16, :] = other.astype(jnp.bfloat16)
+        out_ref[0, :, place : place + 16, :] = low.astype(jnp.bfloat16)
+        out_ref[1, :, place : place + 16, :] = high.astype(jnp.bfloat16)
 
 
 def cross_power(got):
     sources, pairs, lines, rows = got.shape
     every = sources // PAIR * 2 * pairs
-    shape = (every // 8, 2 * lines, every)
+    shape = (CORES, every // 8, 2 * lines, every)
     whole = pl.BlockSpec(memory_space=pltpu.VMEM)
     return pl.pallas_call(
         csd_kernel,
         in_specs=[whole],
-        out_specs=[whole, whole],
-        out_shape=[
-            jax.ShapeDtypeStruct(shape, jnp.float32),
-            jax.ShapeDtypeStruct(shape, jnp.bfloat16),
-        ],
+        out_specs=whole,
+        out_shape=jax.ShapeDtypeStruct(shape, jnp.bfloat16),
         scratch_shapes=[pltpu.VMEM((PAIR, lines // 2, every, rows), jnp.bfloat16)],
         compiler_params=pltpu.CompilerParams(vmem_limit_bytes=VMEM),
         name="csd",
@@ -280,8 +275,8 @@
     rim = shifted(packed_rim(snapshots[:, :RIM].astype(jnp.bfloat16)), "tm", -1)
     begun = early_spectra(snapshots, weights, block_delay, dft_rows(groups), targets, total_rows)
     spectra = late_spectra(*begun, rim)
-    own, other = cross_power(exchange(spectra, ("half", "tm")))
-    pair = (own + shifted(other, "core", 1).astype(jnp.float32)).astype(jnp.bfloat16)
+    halves = exchange(cross_power(exchange(spectra, ("half", "tm"))), "core")
+    pair = jnp.sum(halves.astype(jnp.float32), axis=0).astype(jnp.bfloat16)
     got = exchange(pair, ("half", "chip"))
     return totals(got.reshape((PAIR, chips) + got.shape[1:]), NF // groups)
 

time: 96.9 us -> 97.7 us (level)
  blocking collectives: 71.5 us -> 78.3 us
  starting transfers between devices: 13.5 us -> 8.39 us
    all_to_all x2 -> x3, blocking collectives: 71.5 us -> 78.3 us  [exchange(): return lax.all_to_all(array, axes, split_axis=0, concat_axis=0, tiled=True)]
    ppermute x2 -> x1, starting transfers between devices: 13.5 us -> 8.39 us  [shifted(): lax.ppermute(array, axis, [(i, (i + by) % count) for i in range(count)])]
  transfers between devices with their start and end apart: 2 -> 1, of which waited for: 1 -> 0; matrix products, arithmetic and copies ran while one was open for 0% -> 0% of each run, Pallas kernels for 3% -> 3%
where the time goes in v5:
time: 97.7 us; the launch traced here: 97 us
  blocking collectives  78.3 us (80%)
  starting transfers between devices  8.39 us (9%)
  Pallas kernels  5.29 us (5%)
  local copies, waits for them, and re-layouts  4.92 us (5%)
    all_to_all x3, blocking collectives, exchange(): return lax.all_to_all(array, axes, split_axis=0, concat_axis=0, tiled=True)  78.3 us
    ppermute x1, starting transfers between devices, shifted(): lax.ppermute(array, axis, [(i, (i + by) % count) for i in range(count)])  8.39 us
    unnamed x8, local copies, waits for them, and re-layouts  3.85 us
    pallas_call x1, Pallas kernels, early_spectra(): pl.pallas_call(lambda *refs: early_kernel(total_rows, *refs), grid=(rows...  2.67 us
  transfers between devices with their start and end apart: 1, of which 0 were waited for; matrix products, arithmetic and copies ran while one was open for 0% of the time, Pallas kernels for 3%

profile of v5, /device:TPU:1, one launch (start us, length us, event | category | flops | bytes accessed | tf_op | source)
XLA Modules:
  0.0 97.0 jit_solution(739863563245692553)
XLA Ops:
  0.0 1.1 %slice.7.edge_ref = bf16[512,192]{1,0:T(8,128)(2,1)S(1)} slice(f32[512,1024]{1,0:T(8,128)} %refs_3_.1), slice={[0:512], [0:192]} | slice | bytes 393216 | tf_op jit(solution)/shard_map/slice | solution.py:275
  1.1 0.1 rim.1
  1.2 8.4 %collective-permute-start = (bf16[768,128]{1,0:T(8,128)(2,1)S(1)}, bf16[768,128]{1,0:T(8,128)(2,1)S(1)}, u32[]{:S(2)}, u32[]{:S(2)}) collective-permute-start(bf16[768,128]{1,0:T(8,128)(2,1)S(1)} %rim.1), channel_id=1, source_target_pairs={{0,15},{1,0},{2,1},{3,2},{4,3},{5,4},{6,5},{7,6},{8,7},{9,8},{10,9... | collective-permute-start | bytes 589832 | tf_op jit(solution)/shard_map/ppermute | solution.py:24
  9.6 0.0 copy-start
  9.6 1.6 %copy-done = f32[512,1024]{1,0:T(8,128)S(1)} copy-done((f32[512,1024]{1,0:T(8,128)S(1)}, f32[512,1024]{1,0:T(8,128)}, u32[]{:S(2)}) %copy-start) | copy-done | bytes 2097176
  11.2 0.0 copy-start.1
  11.2 0.9 copy-done.1
  12.1 0.0 copy-start.2
  12.1 0.7 copy-done.2
  12.8 0.0 copy-start.3
  12.8 0.7 copy-done.3
  13.4 2.7 %dft_early.1 = (bf16[32,4,16,512]{3,2,1,0:T(8,128)(2,1)S(1)}, bf16[512,256]{1,0:T(8,128)(2,1)S(1)}, bf16[2,256,384]{2,1,0:T(8,128)(2,1)S(1)}, f32[1,512]{1,0:T(1,128)S(1)}) custom-call(s32[8]{0:T(128)S(1)} %copy-done.3, bf16[256,384]{1,0:T(8,128)(2,1)S(1)} %copy-done.1, f32[1,512]{1,0:T(1,128)S(1)} %bitcast.3, f32[512,1024]{1,0:T(8,128)S(1)} %copy-done), custom_call_target="tpu_custom_call" | custom-call | flops 603979776 | bytes 3670016 | tf_op jit(solution)/shard_map/dft_early/pallas_call | solution.py:101
  16.1 0.0 collective-permute-done.rim_ref
  16.1 0.5 dft_late.1
  16.6 53.9 %all_to_all.15.got_ref = bf16[32,4,16,512]{3,2,1,0:T(8,128)(2,1)S(1)} all-to-all(bf16[32,4,16,512]{3,2,1,0:T(8,128)(2,1)S(1)} %dft_late.1), channel_id=1, replica_groups=mesh['half'=2,'chip'=8,'core'=2,'tm'=16] {'half','tm'}, dimensions={0} | all-to-all | bytes 4194304 | tf_op jit(solution)/shard_map/all_to_all | solution.py:273
  70.5 1.4 %csd.1 = bf16[2,16,32,128]{3,2,1,0:T(8,128)(2,1)S(1)} custom-call(bf16[32,4,16,512]{3,2,1,0:T(8,128)(2,1)S(1)} %all_to_all.15.got_ref), custom_call_target="tpu_custom_call" | custom-call | tf_op jit(solution)/shard_map/csd/pallas_call | solution.py:228
  71.9 6.8 %all_to_all.16 = bf16[2,16,32,128]{3,2,1,0:T(8,128)(2,1)S(1)} all-to-all(bf16[2,16,32,128]{3,2,1,0:T(8,128)(2,1)S(1)} %csd.1), channel_id=1, replica_groups=mesh['half'=2,'chip'=8,'core'=2,'tm'=16] {'core'}, dimensions={0} | all-to-all | bytes 524288 | tf_op jit(solution)/shard_map/all_to_all | solution.py:273
  78.8 17.6 %all_to_all.17 = bf16[16,32,128]{2,1,0:T(8,128)(2,1)S(1)} all-to-all(bf16[16,32,128]{2,1,0:T(8,128)(2,1)S(1)} %reduce_sum.12), channel_id=1, replica_groups=mesh['half'=2,'chip'=8,'core'=2,'tm'=16] {'half','chip'}, dimensions={0} | all-to-all | bytes 262144 | tf_op jit(solution)/shard_map/all_to_all | solution.py:273
  96.4 0.7 total.1
  (1 shorter events, 0.0 us)
Async XLA Ops:
  1.2 14.9 %collective-permute-start = (bf16[768,128]{1,0:T(8,128)(2,1)S(1)}, bf16[768,128]{1,0:T(8,128)(2,1)S(1)}, u32[]{:S(2)}, u32[]{:S(2)}) collective-permute-start(bf16[768,128]{1,0:T(8,128)(2,1)S(1)} %rim.1), channel_id=1, source_target_pairs={{0,15},{1,0},{2,1},{3,2},{4,3},{5,4},{6,5},{7,6},{8,7},{9,8},{10,9... | collective-permute-start | bytes 589832 | tf_op jit(solution)/shard_map/ppermute | solution.py:24
  9.6 1.6 %copy-start = (f32[512,1024]{1,0:T(8,128)S(1)}, f32[512,1024]{1,0:T(8,128)}, u32[]{:S(2)}) copy-start(f32[512,1024]{1,0:T(8,128)} %refs_3_.1) | copy-start | bytes 6291460
  11.2 0.9 copy-start.1
  12.1 0.7 copy-start.2
  12.8 0.7 copy-start.3

commit v6 on v4

--- a/solution.py
+++ b/solution.py
@@ -31,7 +31,7 @@
     norm = np.sqrt(np.sum(window * window))
     table = np.stack([window[:, None] * np.cos(angles), -window[:, None] * np.sin(angles)])
     table = (table / norm).reshape(2, NFFT, groups, PAIR, NF // groups // PAIR)
-    rows = table.transpose(2, 3, 0, 4, 1).reshape(2 * NF, NFFT)
+    rows = table.transpose(3, 2, 0, 4, 1).reshape(2 * NF, NFFT)
     rows = np.pad(rows, ((0, 0), (0, REACH - NFFT)))
     return jnp.asarray(rows, jnp.float32).astype(jnp.bfloat16)
 
@@ -190,14 +190,14 @@
 
 def csd_kernel(order_ref, got_ref, own_ref, other_ref, sorted_ref):
     lines, every, _ = sorted_ref.shape
-    sources, _, _, _, rows = got_ref.shape
+    _, sources, _, _, rows = got_ref.shape
     some = SORTED // lines
     step = sources * some // every
     for half in range(PAIR):
         for k in range(sources // step):
             by_line = lax.dot_general(
                 order_ref[...],
-                got_ref[k * step : (k + 1) * step, half].reshape(some * lines, rows),
+                got_ref[half, k * step : (k + 1) * step].reshape(some * lines, rows),
                 (((1,), (0,)), ((), ())),
                 preferred_element_type=jnp.float32,
             )
@@ -220,7 +220,7 @@
 
 
 def cross_power(order, got):
-    sources, _, pairs, lines, rows = got.shape
+    _, sources, pairs, lines, rows = got.shape
     every = sources * 2 * pairs
     shape = (every // 8, 2 * lines, every)
     whole = pl.BlockSpec(memory_space=pltpu.VMEM)
@@ -280,8 +280,8 @@
         snapshots, scale, block_delay, dft_rows(groups), targets
     )
     spectra = late_spectra(begun, tail, table, scale, rim)
-    received = exchange(spectra, ("tm", "half"))
-    received = received.reshape((groups, PAIR) + received.shape[1:])
+    received = exchange(spectra, ("half", "tm"))
+    received = received.reshape((PAIR, groups) + received.shape[1:])
     own, other = cross_power(order, received)
     pair = (own + shifted(other, "core", 1).astype(jnp.float32)).astype(jnp.bfloat16)
     got = exchange(pair, ("half", "chip"))

time: 97.4 us -> 96.8 us (level)
  no operation moved by 1% of the time
where the time goes in v6:
time: 96.8 us; the launch traced here: 96.2 us
  blocking collectives  72.3 us (75%)
  starting transfers between devices  13.5 us (14%)
  Pallas kernels  4.38 us (5%)
  local copies, waits for them, and re-layouts  4.24 us (4%)
  waiting for transfers between devices  0.97 us (1%)
    all_to_all x2, blocking collectives, exchange(): return lax.all_to_all(array, axes, split_axis=0, concat_axis=0, tiled=True)  72.3 us
    ppermute x2, starting transfers between devices, shifted(): lax.ppermute(array, axis, [(i, (i + by) % count) for i in range(count)])  13.5 us
    unnamed x6, local copies, waits for them, and re-layouts  3.18 us
  transfers between devices with their start and end apart: 2, of which 1 were waited for; matrix products, arithmetic and copies ran while one was open for 1% of the time, Pallas kernels for 2%

profile of v6, /device:TPU:1, one launch (start us, length us, event | category | flops | bytes accessed | tf_op | source)
XLA Modules:
  0.0 96.2 jit_solution(15549865933091012318)
XLA Ops:
  0.0 1.1 %slice.7.edge_ref = bf16[512,192]{1,0:T(8,128)(2,1)S(1)} slice(f32[512,1024]{1,0:T(8,128)} %snap_ref.1), slice={[0:512], [0:192]} | slice | bytes 393216 | tf_op jit(solution)/shard_map/slice | solution.py:277
  1.1 0.1 rim.1
  1.2 8.4 %collective-permute-start = (bf16[768,128]{1,0:T(8,128)(2,1)S(1)}, bf16[768,128]{1,0:T(8,128)(2,1)S(1)}, u32[]{:S(2)}, u32[]{:S(2)}) collective-permute-start(bf16[768,128]{1,0:T(8,128)(2,1)S(1)} %rim.1), channel_id=1, source_target_pairs={{0,15},{1,0},{2,1},{3,2},{4,3},{5,4},{6,5},{7,6},{8,7},{9,8},{10,9... | collective-permute-start | bytes 589832 | tf_op jit(solution)/shard_map/ppermute | solution.py:24
  9.6 0.7 multiply_sqrt_fusion
  10.2 0.0 copy-start
  10.3 1.6 %copy-done = f32[512,1024]{1,0:T(8,128)S(1)} copy-done((f32[512,1024]{1,0:T(8,128)S(1)}, f32[512,1024]{1,0:T(8,128)}, u32[]{:S(2)}) %copy-start) | copy-done | bytes 2097176
  11.8 0.0 copy-start.1
  11.8 0.9 copy-done.1
  12.8 0.0 copy-start.2
  12.8 0.7 copy-done.2
  13.4 1.9 %dft_early.1 = (bf16[32,4,16,512]{3,2,1,0:T(8,128)(2,1)S(1)}, bf16[512,256]{1,0:T(8,128)(2,1)S(1)}, bf16[2,256,384]{2,1,0:T(8,128)(2,1)S(1)}, bf16[256,256]{1,0:T(8,128)(2,1)S(1)}) custom-call(s32[8]{0:T(128)S(1)} %copy-done.2, bf16[256,384]{1,0:T(8,128)(2,1)S(1)} %copy-done.1, f32[1,512]{1,0:T(1,128)S(1)} %bitcast.5, f32[512,1024]{1,0:T(8,128)S(1)} %copy-done), custom_call_target="tpu_custom_call" | custom-call | flops 603979776 | bytes 3670016 | tf_op jit(solution)/shard_map/dft_early/pallas_call | solution.py:108
  15.3 0.0 collective-permute-done.rim_ref
  15.3 0.5 dft_late.1
  15.8 54.7 %all_to_all.10 = bf16[32,4,16,512]{3,2,1,0:T(8,128)(2,1)S(1)} all-to-all(bf16[32,4,16,512]{3,2,1,0:T(8,128)(2,1)S(1)} %dft_late.1), channel_id=1, replica_groups=mesh['half'=2,'chip'=8,'core'=2,'tm'=16] {'half','tm'}, dimensions={0} | all-to-all | bytes 4194304 | tf_op jit(solution)/shard_map/all_to_all | solution.py:275
  70.5 1.3 %csd.1 = (f32[16,32,128]{2,1,0:T(8,128)S(1)}, bf16[16,32,128]{2,1,0:T(8,128)(2,1)S(1)}) custom-call(bf16[256,256]{1,0:T(8,128)(2,1)S(1)} %get-tuple-element.11.order_ref, bf16[2,16,4,16,512]{4,3,2,1,0:T(8,128)(2,1)S(1)} %bitcast.3), custom_call_target="tpu_custom_call" | custom-call | tf_op jit(solution)/shard_map/csd/pallas_call | solution.py:227
  71.7 5.1 %collective-permute-start.1 = (bf16[16,32,128]{2,1,0:T(8,128)(2,1)S(1)}, bf16[16,32,128]{2,1,0:T(8,128)(2,1)S(1)}, u32[]{:S(2)}, u32[]{:S(2)}) collective-permute-start(bf16[16,32,128]{2,1,0:T(8,128)(2,1)S(1)} %get-tuple-element.16), channel_id=1, source_target_pairs={{0,16},{16,0},{1,17},{17,1},{2,18},{18,2},{3,19},{19,3},{4,20},{20... | collective-permute-start | bytes 393224 | tf_op jit(solution)/shard_map/ppermute | solution.py:24
  76.9 1.0 %collective-permute-done.1 = bf16[16,32,128]{2,1,0:T(8,128)(2,1)S(1)} collective-permute-done((bf16[16,32,128]{2,1,0:T(8,128)(2,1)S(1)}, bf16[16,32,128]{2,1,0:T(8,128)(2,1)S(1)}, u32[]{:S(2)}, u32[]{:S(2)}) %collective-permute-start.1) | collective-permute-done | bytes 131104 | tf_op jit(solution)/shard_map/ppermute | solution.py:24
  77.9 17.6 %all_to_all.11 = bf16[16,32,128]{2,1,0:T(8,128)(2,1)S(1)} all-to-all(bf16[16,32,128]{2,1,0:T(8,128)(2,1)S(1)} %add_convert_fusion), channel_id=1, replica_groups=mesh['half'=2,'chip'=8,'core'=2,'tm'=16] {'half','chip'}, dimensions={0} | all-to-all | bytes 262144 | tf_op jit(solution)/shard_map/all_to_all | solution.py:275
  95.5 0.7 total.1
  (1 shorter events, 0.0 us)
Async XLA Ops:
  1.2 14.2 %collective-permute-start = (bf16[768,128]{1,0:T(8,128)(2,1)S(1)}, bf16[768,128]{1,0:T(8,128)(2,1)S(1)}, u32[]{:S(2)}, u32[]{:S(2)}) collective-permute-start(bf16[768,128]{1,0:T(8,128)(2,1)S(1)} %rim.1), channel_id=1, source_target_pairs={{0,15},{1,0},{2,1},{3,2},{4,3},{5,4},{6,5},{7,6},{8,7},{9,8},{10,9... | collective-permute-start | bytes 589832 | tf_op jit(solution)/shard_map/ppermute | solution.py:24
  10.2 1.6 %copy-start = (f32[512,1024]{1,0:T(8,128)S(1)}, f32[512,1024]{1,0:T(8,128)}, u32[]{:S(2)}) copy-start(f32[512,1024]{1,0:T(8,128)} %snap_ref.1) | copy-start | bytes 6291460
  11.8 0.9 copy-start.1
  12.8 0.7 copy-start.2
  71.7 6.1 %collective-permute-start.1 = (bf16[16,32,128]{2,1,0:T(8,128)(2,1)S(1)}, bf16[16,32,128]{2,1,0:T(8,128)(2,1)S(1)}, u32[]{:S(2)}, u32[]{:S(2)}) collective-permute-start(bf16[16,32,128]{2,1,0:T(8,128)(2,1)S(1)} %get-tuple-element.16), channel_id=1, source_target_pairs={{0,16},{16,0},{1,17},{17,1},{2,18},{18,2},{3,19},{19,3},{4,20},{20... | collective-permute-start | bytes 393224 | tf_op jit(solution)/shard_map/ppermute | solution.py:24

commit v7 on v6

--- a/solution.py
+++ b/solution.py
@@ -135,7 +135,7 @@
     )(block_delay, table, scale, snapshots)
 
 
-def late_kernel(table_ref, scale_ref, tail_ref, rim_ref, begun_ref, out_ref):
+def late_kernel(table_ref, scale_ref, tail_ref, rim_ref, begun_ref, out_ref, made_ref, sems):
     rows, _ = tail_ref.shape
     half = RIM - LANES
     rest = rim_ref[rows:].astype(jnp.float32)
@@ -143,16 +143,29 @@
     last = jnp.concatenate([rest, pltpu.roll(rest, half, 1)], axis=0)
     last = jnp.where(lane < half, last, 0.0).astype(jnp.bfloat16)
     pieces = [tail_ref[:, :HOP], tail_ref[:, HOP:], rim_ref[:rows], last]
-    two = []
-    for block in range(table_ref.shape[0]):
-        products = lax.dot_general(
-            table_ref[block],
-            jnp.concatenate(pieces[block : block + REACH // HOP], axis=1),
-            (((1,), (1,)), ((), ())),
-            preferred_element_type=jnp.float32,
+    pairs = out_ref.shape[1]
+    steps, targets, _, strip = made_ref.shape
+    copies = []
+    for s in range(steps):
+        part = slice(s * strip, (s + 1) * strip)
+        two = []
+        for block in range(table_ref.shape[0]):
+            products = lax.dot_general(
+                table_ref[block],
+                jnp.concatenate([p[part] for p in pieces[block : block + REACH // HOP]], axis=1),
+                (((1,), (1,)), ((), ())),
+                preferred_element_type=jnp.float32,
+            )
+            two.append((products * scale_ref[:, part]).reshape(targets, -1, strip))
+        made_ref[s] = jnp.concatenate(two, axis=1).astype(jnp.bfloat16)
+        copies.append(
+            pltpu.make_async_copy(
+                made_ref.at[s], out_ref.at[:, pairs - 1, :, s * strip : (s + 1) * strip], sems.at[s]
+            )
         )
-        two.append((products * scale_ref[...]).reshape(out_ref.shape[0], -1, rows))
-    out_ref[:, 0] = jnp.concatenate(two, axis=1).astype(jnp.bfloat16)
+        copies[-1].start()
+    for copy in copies:
+        copy.wait()
 
 
 def late_spectra(begun, tail, table, scale, rim):
@@ -161,13 +174,14 @@
     whole = pl.BlockSpec(memory_space=pltpu.VMEM)
     return pl.pallas_call(
         late_kernel,
-        grid=(1,),
         in_specs=[whole, whole, whole, whole, pl.BlockSpec(memory_space=pl.ANY)],
-        out_specs=pl.BlockSpec(
-            (targets, late // 2, lines, rows), lambda s: (0, 2 * pairs // late - 1, 0, 0)
-        ),
+        out_specs=pl.BlockSpec(memory_space=pl.ANY),
         out_shape=jax.ShapeDtypeStruct(begun.shape, begun.dtype),
         input_output_aliases={4: 0},
+        scratch_shapes=[
+            pltpu.VMEM((2, targets, lines, rows // 2), jnp.bfloat16),
+            pltpu.SemaphoreType.DMA((2,)),
+        ],
         compiler_params=pltpu.CompilerParams(vmem_limit_bytes=VMEM),
         cost_estimate=pl.CostEstimate(
             flops=4 * NF * REACH * rows * late,

time: 96.8 us -> 97.1 us (level)
  no operation moved by 1% of the time
where the time goes in v7:
time: 97.1 us; the launch traced here: 96.5 us
  blocking collectives  72.3 us (74%)
  starting transfers between devices  13.5 us (14%)
  Pallas kernels  4.66 us (5%)
  local copies, waits for them, and re-layouts  4.24 us (4%)
    all_to_all x2, blocking collectives, exchange(): return lax.all_to_all(array, axes, split_axis=0, concat_axis=0, tiled=True)  72.3 us
    ppermute x2, starting transfers between devices, shifted(): lax.ppermute(array, axis, [(i, (i + by) % count) for i in range(count)])  13.5 us
    unnamed x6, local copies, waits for them, and re-layouts  3.18 us
  transfers between devices with their start and end apart: 2, of which 1 were waited for; matrix products, arithmetic and copies ran while one was open for 1% of the time, Pallas kernels for 2%

profile of v7, /device:TPU:1, one launch (start us, length us, event | category | flops | bytes accessed | tf_op | source)
XLA Modules:
  0.0 96.5 jit_solution(10048486438435456005)
XLA Ops:
  0.0 1.1 %slice.7.edge_ref = bf16[512,192]{1,0:T(8,128)(2,1)S(1)} slice(f32[512,1024]{1,0:T(8,128)} %snap_ref.1), slice={[0:512], [0:192]} | slice | bytes 393216 | tf_op jit(solution)/shard_map/slice | solution.py:291
  1.1 0.1 rim.1
  1.2 8.4 %collective-permute-start = (bf16[768,128]{1,0:T(8,128)(2,1)S(1)}, bf16[768,128]{1,0:T(8,128)(2,1)S(1)}, u32[]{:S(2)}, u32[]{:S(2)}) collective-permute-start(bf16[768,128]{1,0:T(8,128)(2,1)S(1)} %rim.1), channel_id=1, source_target_pairs={{0,15},{1,0},{2,1},{3,2},{4,3},{5,4},{6,5},{7,6},{8,7},{9,8},{10,9... | collective-permute-start | bytes 589832 | tf_op jit(solution)/shard_map/ppermute | solution.py:24
  9.6 0.7 multiply_sqrt_fusion
  10.2 0.0 copy-start
  10.3 1.6 %copy-done = f32[512,1024]{1,0:T(8,128)S(1)} copy-done((f32[512,1024]{1,0:T(8,128)S(1)}, f32[512,1024]{1,0:T(8,128)}, u32[]{:S(2)}) %copy-start) | copy-done | bytes 2097176
  11.8 0.0 copy-start.1
  11.8 0.9 copy-done.1
  12.8 0.0 copy-start.2
  12.8 0.7 copy-done.2
  13.4 1.9 %dft_early.1 = (bf16[32,4,16,512]{3,2,1,0:T(8,128)(2,1)S(1)}, bf16[512,256]{1,0:T(8,128)(2,1)S(1)}, bf16[2,256,384]{2,1,0:T(8,128)(2,1)S(1)}, bf16[256,256]{1,0:T(8,128)(2,1)S(1)}) custom-call(s32[8]{0:T(128)S(1)} %copy-done.2, bf16[256,384]{1,0:T(8,128)(2,1)S(1)} %copy-done.1, f32[1,512]{1,0:T(1,128)S(1)} %bitcast.5, f32[512,1024]{1,0:T(8,128)S(1)} %copy-done), custom_call_target="tpu_custom_call" | custom-call | flops 603979776 | bytes 3670016 | tf_op jit(solution)/shard_map/dft_early/pallas_call | solution.py:108
  15.3 0.0 collective-permute-done.rim_ref
  15.3 0.8 dft_late.1
  16.1 54.7 %all_to_all.10 = bf16[32,4,16,512]{3,2,1,0:T(8,128)(2,1)S(1)} all-to-all(bf16[32,4,16,512]{3,2,1,0:T(8,128)(2,1)S(1)} %dft_late.1), channel_id=1, replica_groups=mesh['half'=2,'chip'=8,'core'=2,'tm'=16] {'half','tm'}, dimensions={0} | all-to-all | bytes 4194304 | tf_op jit(solution)/shard_map/all_to_all | solution.py:289
  70.8 1.3 %csd.1 = (f32[16,32,128]{2,1,0:T(8,128)S(1)}, bf16[16,32,128]{2,1,0:T(8,128)(2,1)S(1)}) custom-call(bf16[256,256]{1,0:T(8,128)(2,1)S(1)} %get-tuple-element.11.order_ref, bf16[2,16,4,16,512]{4,3,2,1,0:T(8,128)(2,1)S(1)} %bitcast.3), custom_call_target="tpu_custom_call" | custom-call | tf_op jit(solution)/shard_map/csd/pallas_call | solution.py:241
  72.0 5.1 %collective-permute-start.1 = (bf16[16,32,128]{2,1,0:T(8,128)(2,1)S(1)}, bf16[16,32,128]{2,1,0:T(8,128)(2,1)S(1)}, u32[]{:S(2)}, u32[]{:S(2)}) collective-permute-start(bf16[16,32,128]{2,1,0:T(8,128)(2,1)S(1)} %get-tuple-element.16), channel_id=1, source_target_pairs={{0,16},{16,0},{1,17},{17,1},{2,18},{18,2},{3,19},{19,3},{4,20},{20... | collective-permute-start | bytes 393224 | tf_op jit(solution)/shard_map/ppermute | solution.py:24
  77.2 1.0 collective-permute-done.1
  78.2 17.6 %all_to_all.11 = bf16[16,32,128]{2,1,0:T(8,128)(2,1)S(1)} all-to-all(bf16[16,32,128]{2,1,0:T(8,128)(2,1)S(1)} %add_convert_fusion), channel_id=1, replica_groups=mesh['half'=2,'chip'=8,'core'=2,'tm'=16] {'half','chip'}, dimensions={0} | all-to-all | bytes 262144 | tf_op jit(solution)/shard_map/all_to_all | solution.py:289
  95.8 0.7 total.1
  (1 shorter events, 0.0 us)
Async XLA Ops:
  1.2 14.2 %collective-permute-start = (bf16[768,128]{1,0:T(8,128)(2,1)S(1)}, bf16[768,128]{1,0:T(8,128)(2,1)S(1)}, u32[]{:S(2)}, u32[]{:S(2)}) collective-permute-start(bf16[768,128]{1,0:T(8,128)(2,1)S(1)} %rim.1), channel_id=1, source_target_pairs={{0,15},{1,0},{2,1},{3,2},{4,3},{5,4},{6,5},{7,6},{8,7},{9,8},{10,9... | collective-permute-start | bytes 589832 | tf_op jit(solution)/shard_map/ppermute | solution.py:24
  10.2 1.6 %copy-start = (f32[512,1024]{1,0:T(8,128)S(1)}, f32[512,1024]{1,0:T(8,128)}, u32[]{:S(2)}) copy-start(f32[512,1024]{1,0:T(8,128)} %snap_ref.1) | copy-start | bytes 6291460
  11.8 0.9 copy-start.1
  12.8 0.7 copy-start.2
  72.0 6.1 %collective-permute-start.1 = (bf16[16,32,128]{2,1,0:T(8,128)(2,1)S(1)}, bf16[16,32,128]{2,1,0:T(8,128)(2,1)S(1)}, u32[]{:S(2)}, u32[]{:S(2)}) collective-permute-start(bf16[16,32,128]{2,1,0:T(8,128)(2,1)S(1)} %get-tuple-element.16), channel_id=1, source_target_pairs={{0,16},{16,0},{1,17},{17,1},{2,18},{18,2},{3,19},{19,3},{4,20},{20... | collective-permute-start | bytes 393224 | tf_op jit(solution)/shard_map/ppermute | solution.py:24
